TPU v7x, 128 devices: a whole 4x4x4 slice. The times are simulated.
128 devices in a mesh: gz: 32 (over z, y, x_lo), gy: 4 (over x_hi, core).
Axes of the slice: x: 4 (x_hi: 2, x_lo: 2; x = x_hi * 2 + x_lo), y: 4, z: 4, core: 2. Of those that a mesh axis runs over, the one named last changes fastest.
Arguments:
- fields: bfloat16 [64, 128, 128, 128], P('gz', 'gy'), may hold values from -6 to 6
- cotangent: bfloat16 [64, 128, 128, 128], P('gz', 'gy'), may hold values from -6 to 6
- w_value: bfloat16 [128, 128], replicated, may hold values from -0.5 to 0.5
- w_out: bfloat16 [128, 128], replicated, may hold values from -0.5 to 0.5
- w_query: float32 [3, 128, 128], replicated, may hold values from -5 to 5
- w_key: float32 [3, 128, 128], replicated, may hold values from -5 to 5
Outputs:
- field_grad: bfloat16 [64, 128, 128, 128], P('gz', 'gy')
- value_grad: float32 [128, 128], replicated
- output_grad: float32 [128, 128], replicated
- query_grad: float32 [3, 128, 128], replicated
- key_grad: float32 [3, 128, 128], replicated
All inputs are finite; a program needn't handle non-finite values.
Results may differ from a plain program's by a relative error of at most 0.0095.
Values may be sent and summed in bfloat16 or wider, within the bound.
A program may use at most 128 MiB of HBM per device.

v0:
```python
import math

import jax
import jax.numpy as jnp
from jax import lax
from jax.sharding import PartitionSpec as P

H = 8


epsilon = 1e-06


def attend_one(pooled, query_weight, key_weight):
    channels = pooled.shape[-1]
    head_size = channels // H
    length = pooled.shape[0]
    mean_square = jnp.mean(pooled * pooled, axis=-1, keepdims=True)
    normed = pooled * lax.rsqrt(mean_square + epsilon)
    queries = jnp.dot(normed, query_weight, precision=lax.Precision.HIGHEST).reshape(
        length, H, head_size
    )
    keys_all = jnp.dot(normed, key_weight, precision=lax.Precision.HIGHEST).reshape(
        length, H, head_size
    )
    scores = jnp.einsum(
        "ihd,jhd->hij", queries, keys_all, precision=lax.Precision.HIGHEST
    ) / math.sqrt(head_size)
    return jax.nn.softmax(scores, axis=-1)


def attend_all(means_z, means_y, means_x, w_query, w_key):
    return (
        attend_one(means_z, w_query[0], w_key[0]),
        attend_one(means_y, w_query[1], w_key[1]),
        attend_one(means_x, w_query[2], w_key[2]),
    )


def head_view(field):
    field_shape = field.shape
    return field.reshape(field_shape[:3] + (H, field_shape[3] // H))


def contract(field, matrix, axis):
    if axis == 0:
        pattern = "hij,jbchd->ibchd"
    elif axis == 1:
        pattern = "hij,ajchd->aichd"
    else:
        pattern = "hij,abjhd->abihd"
    result = jnp.einsum(pattern, matrix, head_view(field), preferred_element_type=jnp.float32)
    return result.astype(jnp.bfloat16).reshape(field.shape)


def pair_sum(left_side, right_side, axis):
    if axis == 0:
        pattern = "ibchd,jbchd->hij"
    elif axis == 1:
        pattern = "aichd,ajchd->hij"
    else:
        pattern = "abihd,abjhd->hij"
    return jnp.einsum(
        pattern, head_view(left_side), head_view(right_side), preferred_element_type=jnp.float32
    )


def output_side(mixed, far_cot, w_out):
    channels = mixed.shape[-1]
    flat_mixed = mixed.reshape(-1, channels)
    flat_cot = far_cot.reshape(-1, channels)
    out_part = jnp.einsum("mc,me->ce", flat_mixed, flat_cot, preferred_element_type=jnp.float32)
    grad_mixed = jnp.einsum("me,ce->mc", flat_cot, w_out, preferred_element_type=jnp.float32)
    return (out_part, grad_mixed.astype(jnp.bfloat16).reshape(mixed.shape))


def settle_z(term):
    return lax.psum(term, ("gz", "gy"))


def settle_y(term):
    return lax.psum(term, ("gz", "gy"))


def local(fields, cotangent, w_value, w_out, w_query, w_key):
    local_z, local_y, length_x, channels = fields.shape
    total_z = local_z * lax.axis_size("gz")
    total_y = local_y * lax.axis_size("gy")
    start_z = lax.axis_index("gz") * local_z
    start_y = lax.axis_index("gy") * local_y
    flat_fields = fields.reshape(-1, channels)
    values = (
        jnp.dot(flat_fields, w_value, preferred_element_type=jnp.float32)
        .astype(jnp.bfloat16)
        .reshape(fields.shape)
    )
    sum_z = jnp.sum(fields, axis=(1, 2), dtype=jnp.float32)
    sum_y = jnp.sum(fields, axis=(0, 2), dtype=jnp.float32)
    sum_x = jnp.sum(fields, axis=(0, 1), dtype=jnp.float32)
    placed_z = lax.dynamic_update_slice(
        jnp.zeros((total_z, channels), jnp.float32), sum_z, (start_z, start_z * 0)
    )
    placed_y = lax.dynamic_update_slice(
        jnp.zeros((total_y, channels), jnp.float32), sum_y, (start_y, start_y * 0)
    )
    pooled_z, pooled_y, pooled_x = lax.psum((placed_z, placed_y, sum_x), ("gz", "gy"))
    means_z = pooled_z / (total_y * length_x)
    means_y = pooled_y / (total_z * length_x)
    means_x = pooled_x / (total_z * total_y)
    attn_z, attn_y, attn_x = attend_all(means_z, means_y, means_x, w_query, w_key)
    kernel_z = attn_z.astype(jnp.bfloat16)
    kernel_y = attn_y.astype(jnp.bfloat16)
    kernel_x = attn_x.astype(jnp.bfloat16)
    back_kernel_z = jnp.swapaxes(kernel_z, 1, 2)
    back_kernel_y = jnp.swapaxes(kernel_y, 1, 2)
    back_kernel_x = jnp.swapaxes(kernel_x, 1, 2)
    after_x = contract(values, kernel_x, 2)
    moved_x, moved_cot = (
        lax.all_to_all(after_x, "gy", split_axis=2, concat_axis=1, tiled=True),
        lax.all_to_all(cotangent, "gy", split_axis=2, concat_axis=1, tiled=True),
    )
    after_y = contract(moved_x, kernel_y, 1)
    whole_y, far_cot = (
        lax.all_to_all(after_y, "gz", split_axis=1, concat_axis=0, tiled=True),
        lax.all_to_all(moved_cot, "gz", split_axis=1, concat_axis=0, tiled=True),
    )
    mixed = contract(whole_y, kernel_z, 0)
    out_part, grad_mixed = output_side(mixed, far_cot, w_out)
    score_z = settle_z(pair_sum(grad_mixed, whole_y, 0))
    grad_y_here = contract(grad_mixed, back_kernel_z, 0)
    grad_y = lax.all_to_all(grad_y_here, "gz", split_axis=0, concat_axis=1, tiled=True)
    score_y = settle_y(pair_sum(grad_y, moved_x, 1))
    grad_x_here = contract(grad_y, back_kernel_y, 1)
    grad_x = lax.all_to_all(grad_x_here, "gy", split_axis=1, concat_axis=2, tiled=True)
    score_x_part = pair_sum(grad_x, values, 2)
    grad_values = contract(grad_x, back_kernel_x, 2)
    flat_grad = grad_values.reshape(-1, channels)
    value_part = jnp.einsum("mc,me->ce", flat_fields, flat_grad, preferred_element_type=jnp.float32)
    score_x, value_grad, output_grad = lax.psum((score_x_part, value_part, out_part), ("gz", "gy"))
    unused, pull = jax.vjp(attend_all, means_z, means_y, means_x, w_query, w_key)
    dmean_z, dmean_y, dmean_x, query_grad, key_grad = pull((score_z, score_y, score_x))
    local_dz = lax.dynamic_slice_in_dim(dmean_z, start_z, local_z, 0) / (total_y * length_x)
    local_dy = lax.dynamic_slice_in_dim(dmean_y, start_y, local_y, 0) / (total_z * length_x)
    local_dx = dmean_x / (total_z * total_y)
    direct = jnp.einsum(
        "mc,ec->me", flat_grad, w_value, preferred_element_type=jnp.float32
    ).reshape(fields.shape)
    field_grad = (
        direct
        + local_dz[:, None, None, :]
        + local_dy[None, :, None, :]
        + local_dx[None, None, :, :]
    ).astype(jnp.bfloat16)
    return (field_grad, value_grad, output_grad, query_grad, key_grad)


def solution(mesh):
    placed = (P("gz", "gy", None, None), P("gz", "gy", None, None), P(), P(), P(), P())
    return jax.shard_map(
        local,
        mesh=mesh,
        in_specs=placed,
        out_specs=(P("gz", "gy", None, None), P(), P(), P(), P()),
        check_vma=False,
    )
```

profile of v0, /device:TPU:1, one launch (start us, length us, event | category | flops | bytes accessed | tf_op | source)
XLA Modules:
  0.0 724.5 jit_solution(12272684729806016540)
XLA Ops:
  7.2 4.3 copy.208
  11.5 6.0 all-to-all-start
  21.7 4.1 copy.236
  25.8 3.5 copy.309
  29.3 138.4 %all-reduce.13.cloned.1.call-done = (f32[128,128]{1,0:T(8,128)}, f32[128,128]{1,0:T(8,128)}) async-done(((f32[128,128]{1,0:T(8,128)}, f32[128,128]{1,0:T(8,128)}), (f32[128,128]{1,0:T(8,128)}, f32[128,128]{1,0:T(8,128)})) %all-reduce.13.cloned.1.call-update) | async-done | bytes 131088 | tf_op jit(solution)/shard_map/psum | solution.py:106
  174.4 4.4 convert_bitcast_fusion.3
  178.7 3.5 copy.239
  182.3 4.5 copy.240
  186.8 5.6 all-to-all-start.4
  192.4 2.9 copy.210
  197.4 21.4 %all-to-all-done.4 = bf16[2,32,128,128]{3,1,0,2:T(8,128)(2,1)} async-done(((bf16[2,32,128,128]{3,1,0,2:T(8,128)(2,1)}), bf16[2,32,128,128]{3,1,0,2:T(8,128)(2,1)}, u32[]{:S(2)}, u32[]{:S(2)}) %all-to-all-start.4) | async-done | bytes 2097184 | tf_op jit(solution)/shard_map/all_to_all | solution.py:119
  218.9 4.8 all-to-all-start.1
  224.1 81.3 %psum.56 = f32[64,128]{1,0:T(8,128)S(1)} all-reduce(f32[64,128]{1,0:T(8,128)S(1)} %constant_dynamic-update-slice_fusion.1), channel_id=1, replica_groups=mesh['gz'=32,'gy'=4] {'gz','gy'}, use_global_device_ids=true, to_apply=%region_1.0 | all-reduce | flops 8192 | bytes 65536 | tf_op jit(solution)/shard_map/psum | solution.py:106
  309.8 11.3 %copy.242 = bf16[2,4,32,32,128]{2,1,4,3,0:T(4,128)(2,1)} copy(bf16[2,4,32,32,128]{4,2,0,3,1:T(8,128)(2,1)} %bitcast.52) | data formatting | bytes 4194304 | tf_op jit(solution)/shard_map/all_to_all | solution.py:119
  321.1 10.6 %reshape.182 = bf16[2,128,32,8,16]{1,4,3,2,0:T(8,128)(2,1)} reshape(bf16[2,4,32,32,128]{2,1,4,3,0:T(4,128)(2,1)} %copy.242) | data formatting | bytes 4194304 | tf_op jit(solution)/shard_map/reshape | solution.py:42
  331.6 3.9 convert_bitcast_fusion.2
  335.5 3.5 copy.245
  339.1 4.6 copy.246
  343.6 4.8 all-to-all-start.5
  356.8 4.1 copy.214
  360.9 9.4 %reshape_reshape.14 = bf16[64,4,32,8,16]{2,1,0,4,3:T(4,128)(2,1)} reshape(bf16[8192,128]{0,1:T(8,128)(2,1)} %copy.214) | data formatting | bytes 4194304 | tf_op jit(solution)/shard_map/reshape;reshape | solution.py:42
  370.3 12.8 %copy.217 = bf16[64,4,32,8,16]{0,2,4,1,3:T(8,128)(2,1)} copy(bf16[64,4,32,8,16]{2,1,0,4,3:T(4,128)(2,1)} %reshape_reshape.14) | data formatting | bytes 4194304 | tf_op jit(solution)/shard_map/reshape;reshape | solution.py:42
  383.1 5.4 convert_bitcast_fusion.1
  388.5 5.8 copy.219
  394.3 5.6 copy.220
  399.9 7.8 %all-to-all-start.2 = ((bf16[64,4,32,128]{3,2,1,0:T(8,128)(2,1)}), bf16[64,4,32,128]{3,2,1,0:T(8,128)(2,1)}, u32[]{:S(2)}, u32[]{:S(2)}) async-start(bf16[64,4,32,128]{3,2,1,0:T(8,128)(2,1)} %copy.220), calls=%async_computation.2 | async-start | bytes 4194304 | tf_op jit(solution)/shard_map/all_to_all | solution.py:131
  408.9 7.8 %copy.248 = bf16[32,2,4,32,128]{3,4,2,1,0:T(8,128)(2,1)} copy(bf16[32,2,4,32,128]{4,3,1,2,0:T(8,128)(2,1)} %bitcast.58) | data formatting | bytes 4194304 | tf_op jit(solution)/shard_map/all_to_all | solution.py:124
  416.7 11.7 %copy.250 = bf16[64,4,32,8,16]{0,2,4,1,3:T(8,128)(2,1)} copy(bf16[64,4,32,8,16]{2,4,3,1,0:T(8,128)(2,1)} %bitcast.246) | data formatting | bytes 4194304 | tf_op jit(solution)/shard_map/reshape | solution.py:42
  428.4 6.8 all-to-all-done.2
  435.2 7.8 %copy.221 = bf16[2,32,4,32,128]{3,4,2,1,0:T(8,128)(2,1)} copy(bf16[2,32,4,32,128]{4,3,2,0,1:T(8,128)(2,1)} %bitcast.19) | data formatting | bytes 4194304 | tf_op jit(solution)/shard_map/all_to_all | solution.py:131
  443.0 10.9 %copy.224 = bf16[2,128,32,8,16]{1,4,2,0,3:T(8,128)(2,1)} copy(bf16[2,128,32,8,16]{2,4,3,1,0:T(8,128)(2,1)} %bitcast.247) | data formatting | bytes 4194304 | tf_op jit(solution)/shard_map/reshape | solution.py:42
  453.9 3.9 convert_bitcast_fusion.5
  457.8 3.5 copy.226
  461.4 4.6 copy.227
  466.0 7.4 %all-to-all-start.3 = ((bf16[2,128,32,128]{3,2,0,1:T(8,128)(2,1)}), bf16[2,128,32,128]{3,2,0,1:T(8,128)(2,1)}, u32[]{:S(2)}, u32[]{:S(2)}) async-start(bf16[2,128,32,128]{3,2,0,1:T(8,128)(2,1)} %copy.227), calls=%async_computation.3 | async-start | bytes 4194304 | tf_op jit(solution)/shard_map/all_to_all | solution.py:134
  473.6 5.4 convert_bitcast_fusion
  479.0 12.7 %copy.268 = bf16[64,4,32,8,16]{2,1,0,4,3:T(4,128)(2,1)} copy(bf16[64,4,32,8,16]{0,2,4,1,3:T(8,128)(2,1)} %convert_bitcast_fusion) | data formatting | bytes 4194304 | tf_op jit(solution)/shard_map/convert_element_type | solution.py:53
  491.7 11.7 %reshape_reshape.17 = bf16[8192,128]{0,1:T(8,128)(2,1)} reshape(bf16[64,4,32,8,16]{2,1,0,4,3:T(4,128)(2,1)} %copy.268) | data formatting | bytes 4194304 | tf_op jit(solution)/shard_map/reshape;reshape | solution.py:70
  503.4 3.7 fusion.103
  507.1 4.5 convolution_bitcast_fusion
  513.1 11.3 %copy.229 = bf16[2,32,4,32,128]{3,2,4,1,0:T(4,128)(2,1)} copy(bf16[2,32,4,32,128]{4,3,0,1,2:T(8,128)(2,1)} %bitcast.33) | data formatting | bytes 4194304 | tf_op jit(solution)/shard_map/all_to_all | solution.py:134
  524.4 10.5 %reshape.179 = bf16[2,32,128,8,16]{2,4,3,1,0:T(8,128)(2,1)} reshape(bf16[2,32,4,32,128]{3,2,4,1,0:T(4,128)(2,1)} %copy.229) | data formatting | bytes 4194304 | tf_op jit(solution)/shard_map/reshape | solution.py:42
  535.0 3.9 convert_bitcast_fusion.4
  538.9 4.8 fusion.21
  545.6 4.4 reshape_reshape.16
  549.9 2.9 convolution_bitcast_fusion.7
  553.0 3.5 copy.234
  556.5 144.2 %all-reduce.11.cloned.1.call-done = (f32[8,128,128]{1,2,0:T(8,128)}, f32[8,128,128]{1,2,0:T(8,128)}, f32[8,64,64]{1,2,0:T(8,128)}, f32[128,128]{0,1:T(8,128)}, f32[128,128]{1,0:T(8,128)}) async-done(((f32[8,128,128]{1,2,0:T(8,128)}, f32[8,128,128]{1,2,0:T(8,128)}, f32[8,64,64]{1,2,0:T(8,128)}, f32[128,128]{0,1:T(8,128)}, f32[128,128]{1,0:T(8,128)}), (f32[8,128,128]{1,2,0:T(8,128)}, ...) | async-done | bytes 1310736 | tf_op jit(solution)/shard_map/psum | solution.py:139
  (184 shorter events, 47.0 us)
Async XLA Ops:
  7.2 12.3 %copy-start = (bf16[128,128]{1,0:T(8,128)(2,1)S(1)}, bf16[128,128]{1,0:T(8,128)(2,1)}, u32[]{:S(2)}) copy-start(bf16[128,128]{1,0:T(8,128)(2,1)} %param.8) | copy-start | bytes 98308
  11.4 6.0 copy-start.2
  11.5 175.3 %all-to-all-start = ((bf16[2,32,128,128]{3,1,0,2:T(8,128)(2,1)}), bf16[2,32,128,128]{3,1,0,2:T(8,128)(2,1)}, u32[]{:S(2)}, u32[]{:S(2)}) async-start(bf16[2,32,128,128]{3,1,0,2:T(8,128)(2,1)} %copy.208), calls=%async_computation | async-start | bytes 4194304 | tf_op jit(solution)/shard_map/all_to_all | solution.py:120
  17.4 2.0 copy-start.16
  17.4 150.3 %all-reduce.13.cloned.1.call-start = ((), (), s32[]{:S(2)}) async-start(), calls=%async_computation.7 | async-start | bytes 262144 | tf_op jit(solution)/shard_map/psum | solution.py:106
  19.4 2.0 copy-start.14
  169.3 3.0 copy-start.40
  171.0 1.2 copy-start.18
  173.9 4.8 copy-start.10
  186.8 32.1 %all-to-all-start.4 = ((bf16[2,32,128,128]{3,1,0,2:T(8,128)(2,1)}), bf16[2,32,128,128]{3,1,0,2:T(8,128)(2,1)}, u32[]{:S(2)}, u32[]{:S(2)}) async-start(bf16[2,32,128,128]{3,1,0,2:T(8,128)(2,1)} %copy.240), calls=%async_computation.4 | async-start | bytes 4194304 | tf_op jit(solution)/shard_map/all_to_all | solution.py:119
  197.4 107.9 %copy-start.42 = (f32[128]{0:T(128)S(1)}, f32[128]{0:T(128)}, u32[]{:S(2)}) copy-start(f32[128]{0:T(128)} %get-tuple-element.65) | copy-start | bytes 1540
  197.4 108.5 %copy-start.6 = (f32[128,128]{1,0:T(8,128)S(1)}, f32[128,128]{1,0:T(8,128)}, u32[]{:S(2)}) copy-start(f32[128,128]{1,0:T(8,128)} %get-tuple-element.38) | copy-start | bytes 196612
  218.9 124.7 %all-to-all-start.1 = ((bf16[2,128,32,128]{3,2,0,1:T(8,128)(2,1)}), bf16[2,128,32,128]{3,2,0,1:T(8,128)(2,1)}, u32[]{:S(2)}, u32[]{:S(2)}) async-start(bf16[2,128,32,128]{3,2,0,1:T(8,128)(2,1)} %copy.211), calls=%async_computation.1 | async-start | bytes 4194304 | tf_op jit(solution)/shard_map/all_to_all | solution.py:125
  343.6 56.3 %all-to-all-start.5 = ((bf16[2,128,32,128]{3,2,0,1:T(8,128)(2,1)}), bf16[2,128,32,128]{3,2,0,1:T(8,128)(2,1)}, u32[]{:S(2)}, u32[]{:S(2)}) async-start(bf16[2,128,32,128]{3,2,0,1:T(8,128)(2,1)} %copy.246), calls=%async_computation.5 | async-start | bytes 4194304 | tf_op jit(solution)/shard_map/all_to_all | solution.py:124
  349.4 1.9 copy-start.28
  349.9 1.4 copy-start.30
  351.3 3.5 copy-start.34
  353.4 1.4 copy-start.3
  399.9 35.3 %all-to-all-start.2 = ((bf16[64,4,32,128]{3,2,1,0:T(8,128)(2,1)}), bf16[64,4,32,128]{3,2,1,0:T(8,128)(2,1)}, u32[]{:S(2)}, u32[]{:S(2)}) async-start(bf16[64,4,32,128]{3,2,1,0:T(8,128)(2,1)} %copy.220), calls=%async_computation.2 | async-start | bytes 4194304 | tf_op jit(solution)/shard_map/all_to_all | solution.py:131
  466.0 47.2 %all-to-all-start.3 = ((bf16[2,128,32,128]{3,2,0,1:T(8,128)(2,1)}), bf16[2,128,32,128]{3,2,0,1:T(8,128)(2,1)}, u32[]{:S(2)}, u32[]{:S(2)}) async-start(bf16[2,128,32,128]{3,2,0,1:T(8,128)(2,1)} %copy.227), calls=%async_computation.3 | async-start | bytes 4194304 | tf_op jit(solution)/shard_map/all_to_all | solution.py:134
  473.4 227.4 %all-reduce.11.cloned.1.call-start = ((), (), s32[]{:S(2)}) async-start(), calls=%async_computation.6 | async-start | bytes 2883584 | tf_op jit(solution)/shard_map/psum | solution.py:139
  503.4 3.7 copy-start.1
  507.1 4.5 copy-start.7
  507.1 4.5 copy-start.8
  538.9 4.8 copy-start.4
  549.9 3.0 copy-start.47
  556.5 146.6 %copy-start.25 = (f32[128,8,16]{0,2,1:T(8,128)S(1)}, f32[128,8,16]{0,2,1:T(8,128)}, u32[]{:S(2)}) copy-start(f32[128,8,16]{0,2,1:T(8,128)} %copy-done.24) | copy-start | bytes 196612
  556.5 147.5 %copy-start.23 = (f32[128,8,16]{0,2,1:T(8,128)S(1)}, f32[128,8,16]{0,2,1:T(8,128)}, u32[]{:S(2)}) copy-start(f32[128,8,16]{0,2,1:T(8,128)} %copy-done.22) | copy-start | bytes 196612
  556.5 148.1 %copy-start.13 = (f32[8,64,64]{1,2,0:T(8,128)S(1)}, f32[8,64,64]{1,2,0:T(8,128)}, u32[]{:S(2)}) copy-start(f32[8,64,64]{1,2,0:T(8,128)} %get-tuple-element.53) | copy-start | bytes 393220
  700.8 3.9 copy-start.26
  700.8 3.9 copy-start.31
  701.9 3.3 copy-start.29
  703.1 2.6 copy-start.9
  705.3 0.8 copy-start.21
  705.3 1.8 copy-start.19
  705.7 2.0 copy-start.38
  705.7 2.3 copy-start.17
  705.7 2.6 copy-start.36
  705.7 3.2 copy-start.5
  705.8 4.9 copy-start.15
  705.8 5.2 copy-start.45
  706.1 5.4 copy-start.43
  706.1 5.9 copy-start.41
  706.1 5.9 copy-start.33
  707.0 7.1 copy-start.46
  707.0 7.3 %copy-start.39 = (f32[128]{0:T(128)S(1)}, f32[128]{0:T(128)}, u32[]{:S(2)}) copy-start(f32[128]{0:T(128)} %get-tuple-element.50) | copy-start | bytes 1540
  707.1 7.4 %copy-start.12 = (bf16[2,32,128,8,16]{2,4,3,1,0:T(8,128)(2,1)S(1)}, bf16[2,32,128,8,16]{2,4,3,1,0:T(8,128)(2,1)}, u32[]{:S(2)}) copy-start(bf16[2,32,128,8,16]{2,4,3,1,0:T(8,128)(2,1)} %copy.234) | copy-start | bytes 6291460
  714.4 2.1 copy-start.32
  (8 other events, 5.4 us)
Sparse Core Ops, SparseCore 0:
  23.7 143.9 all-reduce.12
  553.0 147.6 all-reduce.10
where the time goes:
time: 736 us; the launch traced here: 724 us
  waiting for transfers between devices  311 us (42%)
  local copies, waits for them, and re-layouts  205 us (28%)
  blocking collectives  81.3 us (11%)
  matrix products  64.6 us (9%)
  starting transfers between devices  36.6 us (5%)
  between operations  15.2 us (2%)
  other arithmetic  10.5 us (1%)
    psum x1, waiting for transfers between devices, local(): lax.psum((score_x_part, value_part, out_part), ('gz', 'gy'))  144 us
    psum x1, waiting for transfers between devices, local(): lax.psum((placed_z, placed_y, sum_x), ('gz', 'gy'))  138 us
    psum x1, blocking collectives, local(): lax.psum((placed_z, placed_y, sum_x), ('gz', 'gy'))  81.3 us
    reshape x4, local copies, waits for them, and re-layouts, head_view(): return field.reshape(field_shape[:3] + (H, field_shape[3] // H))  43.7 us
    convert_element_type x7, local copies, waits for them, and re-layouts, contract(): return result.astype(jnp.bfloat16).reshape(field.shape)  34.5 us
    dot_general x6, matrix products, contract(): jnp.einsum(pattern, matrix, head_view(field), preferred_element_type=jnp....  26.8 us
    another operation x2, local copies, waits for them, and re-layouts, head_view(): return field.reshape(field_shape[:3] + (H, field_shape[3] // H))  22.2 us
    all_to_all x1, waiting for transfers between devices, local(): lax.all_to_all(after_x, 'gy', split_axis=2, concat_axis=1, tiled=True)  21.4 us
  transfers between devices with their start and end apart: 8, of which 4 were waited for; matrix products, arithmetic and copies ran while one was open for 26% of the time, Pallas kernels for 0%

commit v1 on v0

v1 whole, which is shorter than its diff:
```python
import functools

import jax
import jax.numpy as jnp
from jax import lax
from jax.experimental import pallas as pl
from jax.experimental.pallas import tpu as pltpu
from jax.sharding import PartitionSpec as P

BF = jnp.bfloat16
F32 = jnp.float32
MESH = pl.DeviceIdType.MESH
H = 8
D = 16
C = 128
Z, Y, X = 64, 128, 128
ZL, YL = 2, 32
CELLS = ZL * YL
GZ, GY = 32, 4
EPS = 1e-06
HIGH = lax.Precision.HIGHEST
COUNTS = (Y * X, Z * X, Z * Y)
STARTS = (0, Z, Z + Y)
LENGTHS = (Z, Y, X)
POOLED = Z + Y + X
VMEM = pl.BlockSpec(memory_space=pltpu.VMEM)


def params(**more):
    return pltpu.CompilerParams(vmem_limit_bytes=56 * 2**20, **more)


def dot(a, b):
    return jnp.dot(a, b, preferred_element_type=F32)


def dot_nt(a, b, precision=None):
    return lax.dot_general(
        a, b, (((1,), (1,)), ((), ())), preferred_element_type=F32, precision=precision
    )


def dot_tn(a, b, precision=None):
    return lax.dot_general(
        a, b, (((0,), (0,)), ((), ())), preferred_element_type=F32, precision=precision
    )


def head_stack(block):
    head = lax.broadcasted_iota(jnp.int32, block.shape, 1) % C // D
    zero = jnp.zeros((), block.dtype)
    return jnp.concatenate([jnp.where(head == h, block, zero) for h in range(H)], axis=0)


def pair_lanes(first, second):
    return jnp.concatenate([first, second], axis=1)


def turn_kernel(src, dst):
    dst[...] = jnp.swapaxes(src[...], 0, 1)


def turn(field):
    return pl.pallas_call(
        turn_kernel,
        grid=(4,),
        in_specs=[pl.BlockSpec((16, X, C), lambda i: (i, 0, 0))],
        out_specs=pl.BlockSpec((X, 16, C), lambda i: (0, i, 0)),
        out_shape=jax.ShapeDtypeStruct((X, CELLS, C), BF),
        compiler_params=params(),
    )(field)


def sums_kernel(src, out):
    step = pl.program_id(0)

    @pl.when(step == 0)
    def clear():
        out[...] = jnp.zeros_like(out)

    block = src[...].astype(F32)
    cells = jnp.sum(block, axis=1)
    gz, gy = lax.axis_index("gz"), lax.axis_index("gy")
    out[pl.ds(Z + Y, X), :] += jnp.sum(block, axis=0)
    out[pl.ds(gz * ZL + step // 2, 1), :] += jnp.sum(cells, axis=0, keepdims=True)
    y_start = pl.multiple_of(Z + gy * YL + (step % 2) * 16, 16)
    out[pl.ds(y_start, 16), :] += cells


def sums(fields):
    return pl.pallas_call(
        sums_kernel,
        grid=(4,),
        in_specs=[pl.BlockSpec((16, X, C), lambda i: (i, 0, 0))],
        out_specs=pl.BlockSpec((POOLED, C), lambda i: (0, 0)),
        out_shape=jax.ShapeDtypeStruct((POOLED, C), F32),
        compiler_params=params(),
    )(fields)


def after_kernel(src, w_value, kernel_x, dst, held):
    values = dot(src[...].reshape(16 * X, C), w_value[...]).astype(BF).reshape(16, X, C)
    for t in range(0, 16, 2):
        wide = head_stack(pair_lanes(values[t], values[t + 1]))
        done = dot(kernel_x[...], wide).astype(BF)
        held[t] = done[:, :C]
        held[t + 1] = done[:, C:]
    dst[...] = jnp.swapaxes(held[...], 0, 1)


def after_all(fields, w_value, kernel_x):
    return pl.pallas_call(
        after_kernel,
        grid=(4,),
        in_specs=[
            pl.BlockSpec((16, X, C), lambda i: (i, 0, 0)),
            pl.BlockSpec((C, C), lambda i: (0, 0)),
            pl.BlockSpec((X, H * X), lambda i: (0, 0)),
        ],
        out_specs=pl.BlockSpec((X, 16, C), lambda i: (0, i, 0)),
        out_shape=jax.ShapeDtypeStruct((X, CELLS, C), BF),
        scratch_shapes=[pltpu.VMEM((16, X, C), BF)],
        compiler_params=params(),
    )(fields, w_value, kernel_x)


def home_kernel(grad, src, w_value, back_x, grad_values, score_x, value_grad):
    @pl.when(pl.program_id(0) == 0)
    def clear():
        score_x[...] = jnp.zeros_like(score_x)
        value_grad[...] = jnp.zeros_like(value_grad)

    grad_x = jnp.swapaxes(grad[...], 0, 1)
    flat = src[...].reshape(16 * X, C)
    values = dot(flat, w_value[...]).astype(BF).reshape(16, X, C)
    total = jnp.zeros((H * X, X), F32)
    for t in range(0, 16, 2):
        wide = head_stack(pair_lanes(grad_x[t], grad_x[t + 1]))
        done = dot(back_x[...], wide).astype(BF)
        grad_values[t] = done[:, :C]
        grad_values[t + 1] = done[:, C:]
        total += dot_nt(wide, pair_lanes(values[t], values[t + 1]))
    score_x[...] += total
    value_grad[...] += dot_tn(flat, grad_values[...].reshape(16 * X, C))


def home(grad, fields, w_value, back_x):
    return pl.pallas_call(
        home_kernel,
        grid=(4,),
        in_specs=[
            pl.BlockSpec((X, 16, C), lambda i: (0, i, 0)),
            pl.BlockSpec((16, X, C), lambda i: (i, 0, 0)),
            pl.BlockSpec((C, C), lambda i: (0, 0)),
            pl.BlockSpec((X, H * X), lambda i: (0, 0)),
        ],
        out_specs=[
            pl.BlockSpec((16, X, C), lambda i: (i, 0, 0)),
            pl.BlockSpec((H * X, X), lambda i: (0, 0)),
            pl.BlockSpec((C, C), lambda i: (0, 0)),
        ],
        out_shape=[
            jax.ShapeDtypeStruct((CELLS, X, C), BF),
            jax.ShapeDtypeStruct((H * X, X), F32),
            jax.ShapeDtypeStruct((C, C), F32),
        ],
        compiler_params=params(),
    )(grad, fields, w_value, back_x)


def finish_kernel(grad_values, w_value, means_grad, out):
    step = pl.program_id(0)
    gz, gy = lax.axis_index("gz"), lax.axis_index("gy")
    direct = dot_nt(grad_values[...].reshape(16 * X, C), w_value[...]).reshape(16, X, C)
    part_z = means_grad[pl.ds(gz * ZL + step // 2, 1), :] / COUNTS[0]
    y_start = pl.multiple_of(Z + gy * YL + (step % 2) * 16, 16)
    part_y = means_grad[pl.ds(y_start, 16), :] / COUNTS[1]
    part_x = means_grad[pl.ds(Z + Y, X), :] / COUNTS[2]
    cells = part_z + part_y
    out[...] = (direct + cells[:, None, :] + part_x[None]).astype(BF)


def finish(grad_values, w_value, means_grad):
    return pl.pallas_call(
        finish_kernel,
        grid=(4,),
        in_specs=[
            pl.BlockSpec((16, X, C), lambda i: (i, 0, 0)),
            pl.BlockSpec((C, C), lambda i: (0, 0)),
            pl.BlockSpec((POOLED, C), lambda i: (0, 0)),
        ],
        out_specs=pl.BlockSpec((16, X, C), lambda i: (i, 0, 0)),
        out_shape=jax.ShapeDtypeStruct((CELLS, X, C), BF),
        compiler_params=params(),
    )(grad_values, w_value, means_grad)


def far_back_kernel(cot, w_out, back_z, back_y, cot_y, mixed_y, grad_y, grad_out, held):
    def over_z(step, carry):
        side, start = step // 2, pl.multiple_of((step % 2) * 16, 16)
        block = cot[:, side, :, pl.ds(start, 16), :].reshape(Z, 16, C)
        turned = jnp.swapaxes(block, 0, 1)
        y_start = pl.multiple_of(step * 16, 16)
        cot_y[pl.ds(y_start, 16)] = turned
        grad_mixed = dot_nt(turned.reshape(16 * Z, C), w_out[...]).astype(BF).reshape(16, Z, C)
        mixed_y[pl.ds(y_start, 16)] = grad_mixed
        for t in range(0, 16, 2):
            wide = head_stack(pair_lanes(grad_mixed[t], grad_mixed[t + 1]))
            done = dot(back_z[...], wide).astype(BF)
            held[t] = done[:, :C]
            held[t + 1] = done[:, C:]
        grad_y[:, pl.ds(y_start, 16), :] = jnp.swapaxes(held[...], 0, 1)
        return carry

    lax.fori_loop(0, 8, over_z, 0)

    def over_y(t, carry):
        wide = head_stack(pair_lanes(grad_y[2 * t], grad_y[2 * t + 1]))
        done = dot(back_y[...], wide).astype(BF)
        for side in range(GY):
            for low in range(ZL):
                grad_out[t, side, low] = done[side * YL : (side + 1) * YL, low * C : (low + 1) * C]
        return carry

    lax.fori_loop(0, Z // 2, over_y, 0)


def far_back(cot, w_out, back_z, back_y):
    return pl.pallas_call(
        far_back_kernel,
        in_specs=[VMEM] * 4,
        out_specs=[VMEM] * 4,
        out_shape=[
            jax.ShapeDtypeStruct((Y, Z, C), BF),
            jax.ShapeDtypeStruct((Y, Z, C), BF),
            jax.ShapeDtypeStruct((Z, Y, C), BF),
            jax.ShapeDtypeStruct((GZ, GY, ZL, YL, C), BF),
        ],
        scratch_shapes=[pltpu.VMEM((16, Z, C), BF)],
        compiler_params=params(),
        cost_estimate=pl.CostEstimate(flops=3 * 10**9, bytes_accessed=10 * 2**20, transcendentals=0),
    )(cot, w_out, back_z, back_y)


def far_kernel(after, cot_y, mixed_y, grad_y, kernel_z, kernel_y, score_z, score_y, out_grad, held):
    score_z[...] = jnp.zeros_like(score_z)
    score_y[...] = jnp.zeros_like(score_y)
    out_grad[...] = jnp.zeros_like(out_grad)

    def over_y(t, carry):
        lines = [after[t, :, low].reshape(Y, C) for low in range(ZL)]
        block = pair_lanes(lines[0], lines[1])
        done = dot(kernel_y[...], head_stack(block)).astype(BF)
        held[2 * t] = done[:, :C]
        held[2 * t + 1] = done[:, C:]
        score_y[...] += dot_nt(head_stack(pair_lanes(grad_y[2 * t], grad_y[2 * t + 1])), block)
        return carry

    lax.fori_loop(0, Z // 2, over_y, 0)

    def over_z(step, carry):
        y_start = pl.multiple_of(step * 16, 16)
        after_y = jnp.swapaxes(held[:, pl.ds(y_start, 16), :], 0, 1)
        grad_mixed = mixed_y[pl.ds(y_start, 16)]
        parts = []
        total = jnp.zeros((H * Z, Z), F32)
        for t in range(0, 16, 2):
            block = pair_lanes(after_y[t], after_y[t + 1])
            done = dot(kernel_z[...], head_stack(block)).astype(BF)
            parts += [done[:, :C], done[:, C:]]
            total += dot_nt(head_stack(pair_lanes(grad_mixed[t], grad_mixed[t + 1])), block)
        score_z[...] += total
        mixed = jnp.concatenate(parts, axis=0)
        out_grad[...] += dot_tn(mixed, cot_y[pl.ds(y_start, 16)].reshape(16 * Z, C))
        return carry

    lax.fori_loop(0, 8, over_z, 0)


def far(after, cot_y, mixed_y, grad_y, kernel_z, kernel_y):
    return pl.pallas_call(
        far_kernel,
        in_specs=[VMEM] * 6,
        out_specs=[VMEM] * 3,
        out_shape=[
            jax.ShapeDtypeStruct((H * Z, Z), F32),
            jax.ShapeDtypeStruct((H * Y, Y), F32),
            jax.ShapeDtypeStruct((C, C), F32),
        ],
        scratch_shapes=[pltpu.VMEM((Z, Y, C), BF)],
        compiler_params=params(),
        cost_estimate=pl.CostEstimate(flops=6 * 10**9, bytes_accessed=10 * 2**20, transcendentals=0),
    )(after, cot_y, mixed_y, grad_y, kernel_z, kernel_y)


def normalise(pooled, axis):
    means = pooled[pl.ds(STARTS[axis], LENGTHS[axis]), :] / COUNTS[axis]
    scale = lax.rsqrt(jnp.mean(means * means, axis=-1, keepdims=True) + EPS)
    return means * scale, scale


def project(normed, weight):
    return jnp.dot(normed, weight, preferred_element_type=F32, precision=HIGH)


def maps_kernel(pooled, w_query, w_key, *outs):
    for axis in range(3):
        length = LENGTHS[axis]
        attn, kernel, back = outs[3 * axis : 3 * axis + 3]
        normed, _ = normalise(pooled, axis)
        queries = project(normed, w_query[axis])
        keys = project(normed, w_key[axis])
        scores = dot_nt(head_stack(queries), keys, HIGH) * (1.0 / D**0.5)
        grown = jnp.exp(scores - jnp.max(scores, axis=-1, keepdims=True))
        soft = grown / jnp.sum(grown, axis=-1, keepdims=True)
        attn[...] = soft
        heads = [soft[h * length : (h + 1) * length] for h in range(H)]
        kernel[...] = jnp.concatenate(heads, axis=1).astype(BF)
        back[...] = jnp.concatenate([head.T for head in heads], axis=1).astype(BF)


def maps(pooled, w_query, w_key):
    shapes = []
    for length in LENGTHS:
        shapes += [
            jax.ShapeDtypeStruct((H * length, length), F32),
            jax.ShapeDtypeStruct((length, H * length), BF),
            jax.ShapeDtypeStruct((length, H * length), BF),
        ]
    return pl.pallas_call(
        maps_kernel,
        in_specs=[VMEM] * 3,
        out_specs=[VMEM] * 9,
        out_shape=shapes,
        compiler_params=params(),
    )(pooled, w_query, w_key)


def pull_kernel(pooled, w_query, w_key, attn_z, attn_y, attn_x, score_z, score_y, score_x, value_grad, out_grad, out):
    for axis, (attn, score) in enumerate(((attn_z, score_z), (attn_y, score_y), (attn_x, score_x))):
        length, start = LENGTHS[axis], STARTS[axis]
        normed, _ = normalise(pooled, axis)
        queries = head_stack(project(normed, w_query[axis]))
        keys = head_stack(project(normed, w_key[axis]))
        soft, grad = attn[...], score[...]
        inner = jnp.sum(soft * grad, axis=-1, keepdims=True)
        grad = soft * (grad - inner) * (1.0 / D**0.5)
        heads = [grad[h * length : (h + 1) * length] for h in range(H)]
        out[pl.ds(start, length), :] = jnp.dot(
            jnp.concatenate(heads, axis=1), keys, preferred_element_type=F32, precision=HIGH
        )
        out[pl.ds(POOLED + start, length), :] = dot_tn(grad, queries, HIGH)
    out[pl.ds(2 * POOLED, C), :] = value_grad[...]
    out[pl.ds(2 * POOLED + C, C), :] = out_grad[...]


def pull(pooled, w_query, w_key, attns, scores, value_grad, out_grad):
    return pl.pallas_call(
        pull_kernel,
        in_specs=[VMEM] * 11,
        out_specs=VMEM,
        out_shape=jax.ShapeDtypeStruct((2 * POOLED + 2 * C, C), F32),
        compiler_params=params(),
    )(pooled, w_query, w_key, *attns, *scores, value_grad, out_grad)


def settle_kernel(pooled, w_query, w_key, total, means_grad, query_grad, key_grad, value_grad, out_grad):
    for axis in range(3):
        length, start = LENGTHS[axis], STARTS[axis]
        normed, scale = normalise(pooled, axis)
        grad_q = total[pl.ds(start, length), :]
        grad_k = total[pl.ds(POOLED + start, length), :]
        query_grad[axis] = dot_tn(normed, grad_q, HIGH)
        key_grad[axis] = dot_tn(normed, grad_k, HIGH)
        grad = dot_nt(grad_q, w_query[axis], HIGH) + dot_nt(grad_k, w_key[axis], HIGH)
        inner = jnp.mean(grad * normed, axis=-1, keepdims=True)
        means_grad[pl.ds(start, length), :] = scale * (grad - normed * inner)
    value_grad[...] = total[pl.ds(2 * POOLED, C), :]
    out_grad[...] = total[pl.ds(2 * POOLED + C, C), :]


def settle(pooled, w_query, w_key, total):
    return pl.pallas_call(
        settle_kernel,
        in_specs=[VMEM] * 4,
        out_specs=[VMEM] * 5,
        out_shape=[
            jax.ShapeDtypeStruct((POOLED, C), F32),
            jax.ShapeDtypeStruct((3, C, C), F32),
            jax.ShapeDtypeStruct((3, C, C), F32),
            jax.ShapeDtypeStruct((C, C), F32),
            jax.ShapeDtypeStruct((C, C), F32),
        ],
        compiler_params=params(),
    )(pooled, w_query, w_key, total)


def sum_kernel(src, out, near, wide, near_send, near_recv, wide_send, wide_recv, back_send, back_recv):
    gz, gy = lax.axis_index("gz"), lax.axis_index("gy")
    line, side = gz // 2, (gz % 2) * 4 + gy
    piece = src.shape[0] // 8

    def near_peer(k):
        peer = (side + k) % 8
        return peer, (line * 2 + peer // 4, peer % 4)

    def wide_peer(k):
        peer = (line + k) % 16
        return peer, (peer * 2 + gz % 2, gy)

    barrier = pltpu.get_barrier_semaphore()
    for k in range(1, 8):
        pl.semaphore_signal(barrier, inc=1, device_id=near_peer(k)[1], device_id_type=MESH)
    for k in range(1, 16):
        pl.semaphore_signal(barrier, inc=1, device_id=wide_peer(k)[1], device_id_type=MESH)
    pl.semaphore_wait(barrier, 22)

    def rows(index):
        return pl.ds(pl.multiple_of(index * piece, 8), piece)

    for k in range(1, 8):
        peer, device = near_peer(k)
        pltpu.make_async_remote_copy(
            src.at[rows(peer)], near.at[side], near_send, near_recv, device_id=device, device_id_type=MESH
        ).start()
    near[side] = src[rows(side)]
    sent = near.at[pl.ds(0, 7)]
    pltpu.make_async_copy(sent, sent, near_recv).wait()
    wide[line] = jnp.sum(near[...], axis=0)
    for k in range(1, 16):
        peer, device = wide_peer(k)
        pltpu.make_async_remote_copy(
            wide.at[line], wide.at[line], wide_send, wide_recv, device_id=device, device_id_type=MESH
        ).start()
    sent_wide = wide.at[pl.ds(0, 15)]
    pltpu.make_async_copy(sent_wide, sent_wide, wide_recv).wait()
    out[rows(side)] = jnp.sum(wide[...], axis=0)
    for k in range(1, 8):
        peer, device = near_peer(k)
        pltpu.make_async_remote_copy(
            out.at[rows(side)], out.at[rows(side)], back_send, back_recv, device_id=device, device_id_type=MESH
        ).start()
    pltpu.make_async_copy(sent, sent, back_recv).wait()
    pltpu.make_async_copy(sent, sent, near_send).wait()
    pltpu.make_async_copy(sent_wide, sent_wide, wide_send).wait()
    pltpu.make_async_copy(sent, sent, back_send).wait()


def sum_all(parts, collective_id):
    rows = parts.shape[0]
    return pl.pallas_call(
        sum_kernel,
        in_specs=[VMEM],
        out_specs=VMEM,
        out_shape=jax.ShapeDtypeStruct(parts.shape, F32),
        scratch_shapes=[
            pltpu.VMEM((8, rows // 8, C), F32),
            pltpu.VMEM((16, rows // 8, C), F32),
        ]
        + [pltpu.SemaphoreType.DMA] * 6,
        compiler_params=params(collective_id=collective_id, has_side_effects=True),
    )(parts)


def exchange(blocks):
    return lax.all_to_all(blocks, ("gz", "gy"), split_axis=0, concat_axis=0, tiled=True)


def local(fields, cotangent, w_value, w_out, w_query, w_key):
    fields = fields.reshape(CELLS, X, C)
    far_cot = exchange(turn(cotangent.reshape(CELLS, X, C))).reshape(GZ, GY, ZL, YL, C)
    pooled = sum_all(sums(fields), 0)
    attn_z, kernel_z, back_z, attn_y, kernel_y, back_y, attn_x, kernel_x, back_x = maps(
        pooled, w_query, w_key
    )
    after = exchange(after_all(fields, w_value, kernel_x)).reshape(GZ, GY, ZL, YL, C)
    cot_y, mixed_y, grad_y, grad_out = far_back(far_cot, w_out, back_z, back_y)
    grad_home = exchange(grad_out.reshape(X, CELLS, C))
    score_z, score_y, out_part = far(after, cot_y, mixed_y, grad_y, kernel_z, kernel_y)
    grad_values, score_x, value_part = home(grad_home, fields, w_value, back_x)
    total = sum_all(
        pull(
            pooled, w_query, w_key, (attn_z, attn_y, attn_x), (score_z, score_y, score_x), value_part, out_part
        ),
        1,
    )
    means_grad, query_grad, key_grad, value_grad, out_grad = settle(pooled, w_query, w_key, total)
    field_grad = finish(grad_values, w_value, means_grad).reshape(ZL, YL, X, C)
    return (field_grad, value_grad, out_grad, query_grad, key_grad)


def solution(mesh):
    placed = (P("gz", "gy", None, None), P("gz", "gy", None, None), P(), P(), P(), P())
    return jax.shard_map(
        local,
        mesh=mesh,
        in_specs=placed,
        out_specs=(P("gz", "gy", None, None), P(), P(), P(), P()),
        check_vma=False,
    )
```

time: 736 us -> 197 us (0.27); the launches traced: 724 us -> 196 us
  waiting for transfers between devices: 311 us -> 15.4 us
  local copies, waits for them, and re-layouts: 205 us -> 1.32 us
  Pallas kernels: 0 us -> 155 us
  blocking collectives: 81.3 us -> 0 us
  matrix products: 64.6 us -> 0 us
  between operations: 15.2 us -> 0.69 us
  starting transfers between devices: 36.6 us -> 23.4 us
  other arithmetic: 10.5 us -> 0 us
    psum x2 -> x0, waiting for transfers between devices: 283 us -> none  [the longest x1 144 us: local(): lax.psum((score_x_part, value_part, out_part), ('gz', 'gy'))]
    pallas_call x0 -> x12, Pallas kernels: none -> 155 us  [the longest x2 68.4 us: sum_all(): pl.pallas_call(sum_kernel, in_specs=[VMEM], out_specs=VMEM, out_shape=jax...]
    psum x1 -> x0, blocking collectives: 81.3 us -> none  [local(): lax.psum((placed_z, placed_y, sum_x), ('gz', 'gy'))]
    dot_general x41 -> x0, matrix products: 64.6 us -> none  [the longest x6 26.8 us: contract(): jnp.einsum(pattern, matrix, head_view(field), preferred_element_type=jnp....]
    reshape x8 -> x0, local copies, waits for them, and re-layouts: 63 us -> none  [the longest x4 43.7 us: head_view(): return field.reshape(field_shape[:3] + (H, field_shape[3] // H))]
    all_to_all x7 -> x0, local copies, waits for them, and re-layouts: 45.3 us -> none  [the longest x1 11.3 us: local(): lax.all_to_all(after_x, 'gy', split_axis=2, concat_axis=1, tiled=True)]
    convert_element_type x9 -> x0, local copies, waits for them, and re-layouts: 42.7 us -> none  [the longest x7 34.5 us: contract(): return result.astype(jnp.bfloat16).reshape(field.shape)]
    another operation x4 -> x0, local copies, waits for them, and re-layouts: 38.2 us -> none  [the longest x2 22.2 us: head_view(): return field.reshape(field_shape[:3] + (H, field_shape[3] // H))]
  transfers between devices with their start and end apart: 8 -> 3, of which waited for: 4 -> 2; matrix products, arithmetic and copies ran while one was open for 26% -> 0% of each run, Pallas kernels for 0% -> 49%
where the time goes in v1:
time: 197 us; the launch traced here: 196 us
  Pallas kernels  155 us (79%)
  starting transfers between devices  23.4 us (12%)
  waiting for transfers between devices  15.4 us (8%)
    pallas_call x2, Pallas kernels, sum_all(): pl.pallas_call(sum_kernel, in_specs=[VMEM], out_specs=VMEM, out_shape=jax...  68.4 us
    pallas_call x1, Pallas kernels, far(): pl.pallas_call(far_kernel, in_specs=[VMEM] * 6, out_specs=[VMEM] * 3, out...  25.8 us
    all_to_all x3, starting transfers between devices, exchange(): lax.all_to_all(blocks, ('gz', 'gy'), split_axis=0, concat_axis=0, tiled=T...  23.4 us
    pallas_call x1, Pallas kernels, far_back(): pl.pallas_call(far_back_kernel, in_specs=[VMEM] * 4, out_specs=[VMEM] * 4...  18.5 us
    all_to_all x3, waiting for transfers between devices, exchange(): lax.all_to_all(blocks, ('gz', 'gy'), split_axis=0, concat_axis=0, tiled=T...  15.4 us
    pallas_call x1, Pallas kernels, home(): pl.pallas_call(home_kernel, grid=(4,), in_specs=[pl.BlockSpec((X, 16, C),...  10.6 us
    pallas_call x1, Pallas kernels, after_all(): pl.pallas_call(after_kernel, grid=(4,), in_specs=[pl.BlockSpec((16, X, C)...  6.17 us
    pallas_call x1, Pallas kernels, pull(): pl.pallas_call(pull_kernel, in_specs=[VMEM] * 11, out_specs=VMEM, out_sha...  5.92 us
  transfers between devices with their start and end apart: 3, of which 2 were waited for; matrix products, arithmetic and copies ran while one was open for 0% of the time, Pallas kernels for 49%

profile of v1, /device:TPU:1, one launch (start us, length us, event | category | flops | bytes accessed | tf_op | source)
XLA Modules:
  0.0 195.9 jit_solution(3731689651083388266)
XLA Ops:
  0.6 4.0 %shard_map.101 = bf16[128,64,128]{2,1,0:T(8,128)(2,1)} custom-call(bf16[64,128,128]{2,1,0:T(8,128)(2,1)} %bitcast.9), custom_call_target="tpu_custom_call" | custom-call | tf_op jit(solution)/shard_map/pallas_call | solution.py:64
  4.6 11.5 %all-to-all-start = ((bf16[128,64,128]{2,1,0:T(8,128)(2,1)}), bf16[128,64,128]{2,1,0:T(8,128)(2,1)S(1)}, u32[]{:S(2)}, u32[]{:S(2)}) async-start(bf16[128,64,128]{2,1,0:T(8,128)(2,1)} %shard_map.101), calls=%async_computation | async-start | bytes 4194304 | tf_op jit(solution)/shard_map/all_to_all | solution.py:466
  16.1 3.4 %shard_map.102.src = f32[320,128]{1,0:T(8,128)} custom-call(bf16[64,128,128]{2,1,0:T(8,128)(2,1)} %bitcast.6), custom_call_target="tpu_custom_call" | custom-call | tf_op jit(solution)/shard_map/pallas_call | solution.py:91
  19.5 36.8 %shard_map.103.pooled = f32[320,128]{1,0:T(8,128)} custom-call(f32[320,128]{1,0:T(8,128)} %shard_map.102.src), custom_call_target="tpu_custom_call" | custom-call | tf_op jit(solution)/shard_map/pallas_call | solution.py:451
  56.3 4.6 %shard_map.104 = (f32[512,64]{1,0:T(8,128)}, bf16[64,512]{1,0:T(8,128)(2,1)}, bf16[64,512]{1,0:T(8,128)(2,1)}, f32[1024,128]{1,0:T(8,128)}, bf16[128,1024]{1,0:T...) custom-call(f32[320,128]{1,0:T(8,128)} %shard_map.103.pooled, ...), custom_call_target="tpu_custom_call" | custom-call | tf_op jit(solution)/shard_map/pallas_call | solution.py:330
  60.9 6.2 %shard_map.107 = bf16[128,64,128]{2,1,0:T(8,128)(2,1)} custom-call(bf16[64,128,128]{2,1,0:T(8,128)(2,1)} %bitcast.7, bf16[128,128]{1,0:T(8,128)(2,1)} %w_value.5, bf16[128,1024]{1,0:T(8,128)(2,1)} %get-tuple-element.37.kernel_x), custom_call_target="tpu_custom_call" | custom-call | tf_op jit(solution)/shard_map/pallas_call | solution.py:112
  67.0 0.0 all-to-all-done
  67.0 0.0 copy-start.1
  67.0 7.2 %all-to-all-start.2 = ((bf16[128,64,128]{2,1,0:T(8,128)(2,1)}), bf16[128,64,128]{2,1,0:T(8,128)(2,1)}, u32[]{:S(2)}, u32[]{:S(2)}) async-start(bf16[128,64,128]{2,1,0:T(8,128)(2,1)} %shard_map.107), calls=%async_computation.2 | async-start | bytes 4194304 | tf_op jit(solution)/shard_map/all_to_all | solution.py:466
  74.2 0.0 copy-done.1
  74.2 18.5 %shard_map.105 = (bf16[128,64,128]{2,1,0:T(8,128)(2,1)}, bf16[128,64,128]{2,1,0:T(8,128)(2,1)}, bf16[64,128,128]{2,1,0:T(8,128)(2,1)}, bf16[32,4,2,32,128]{4,3,2,1,0:T(8,128)(2,1)}) custom-call(bf16[32,4,2,32,128]{4,3,2,1,0:T(8,128)(2,1)} %bitcast.10, bf16[128,128]{1,0:T(8,128)(2,1)} %w_out.1, bf16[64,512]{1,0:T(8,128)(2,1)} %get-tuple-element.29.back_z, ...), custom_call_target="tpu_custom_call" | custom-call | flops 3000000000 | bytes 10485760 | tf_op jit(solution)/shard_map/pallas_call | solution.py:229
  92.7 11.1 %all-to-all-done.2 = bf16[128,64,128]{2,1,0:T(8,128)(2,1)} async-done(((bf16[128,64,128]{2,1,0:T(8,128)(2,1)}), bf16[128,64,128]{2,1,0:T(8,128)(2,1)}, u32[]{:S(2)}, u32[]{:S(2)}) %all-to-all-start.2) | async-done | bytes 2097184 | tf_op jit(solution)/shard_map/all_to_all | solution.py:466
  103.8 4.7 %all-to-all-start.1 = ((bf16[128,64,128]{2,1,0:T(8,128)(2,1)}), bf16[128,64,128]{2,1,0:T(8,128)(2,1)S(1)}, u32[]{:S(2)}, u32[]{:S(2)}) async-start(bf16[128,64,128]{2,1,0:T(8,128)(2,1)} %bitcast.11), calls=%async_computation.1 | async-start | bytes 4194304 | tf_op jit(solution)/shard_map/all_to_all | solution.py:466
  108.6 25.8 %shard_map.108 = (f32[512,64]{1,0:T(8,128)}, f32[1024,128]{1,0:T(8,128)}, f32[128,128]{1,0:T(8,128)}) custom-call(bf16[32,4,2,32,128]{4,3,2,1,0:T(8,128)(2,1)} %bitcast.4.after, bf16[128,64,128]{2,1,0:T(8,128)(2,1)} %get-tuple-element.38.cot_y, bf16[128,64,128]{2,1,0:T(8,128)(2,1)} %get-tuple-element.39.mixed_y, ...), custom_call_target="tpu_custom_call" | custom-call | flops 6000000000 | bytes 10485760 | tf_op jit(solution)/shard_map/pallas_call | solution.py:281
  134.3 4.3 %all-to-all-done.1.grad = bf16[128,64,128]{2,1,0:T(8,128)(2,1)S(1)} async-done(((bf16[128,64,128]{2,1,0:T(8,128)(2,1)}), bf16[128,64,128]{2,1,0:T(8,128)(2,1)S(1)}, u32[]{:S(2)}, u32[]{:S(2)}) %all-to-all-start.1) | async-done | bytes 2097184 | tf_op jit(solution)/shard_map/all_to_all | solution.py:466
  138.6 0.0 copy-start
  138.6 1.3 copy-done
  140.0 10.6 %shard_map.106 = (bf16[64,128,128]{2,1,0:T(8,128)(2,1)}, f32[1024,128]{1,0:T(8,128)}, f32[128,128]{1,0:T(8,128)}) custom-call(bf16[128,64,128]{2,1,0:T(8,128)(2,1)} %copy-done, bf16[64,128,128]{2,1,0:T(8,128)(2,1)} %bitcast.8, bf16[128,128]{1,0:T(8,128)(2,1)} %w_value.5, bf16[128,1024]{1,0:T(8,128)(2,1)} %get-tuple-element.32.back_x), custom_call_target="tpu_custom_call" | custom-call | tf_op jit(solution)/shard_map/pallas_call | solution.py:148
  150.5 5.9 %shard_map.109.src = f32[896,128]{1,0:T(8,128)} custom-call(f32[320,128]{1,0:T(8,128)} %shard_map.103.pooled, f32[3,128,128]{2,1,0:T(8,128)} %w_query.5, f32[3,128,128]{2,1,0:T(8,128)} %w_key.5, f32[512,64]{1,0:T(8,128)} %get-tuple-element.34.attn_z, f32[1024,128]{1,0:T(8,128)} %get-tuple-element.35.attn_y, f32[1024,128]{1,0:T(8,128)} %get-tuple-element.36.attn_x, ...), custom_call_target="tpu_custom_call" | custom-call | tf_op jit(solution)/shard_map/pallas_call | solution.py:358
  156.4 31.6 %shard_map.110.total = f32[896,128]{1,0:T(8,128)} custom-call(f32[896,128]{1,0:T(8,128)} %shard_map.109.src), custom_call_target="tpu_custom_call" | custom-call | tf_op jit(solution)/shard_map/pallas_call | solution.py:451
  188.1 3.5 %shard_map.111 = (f32[320,128]{1,0:T(8,128)}, f32[3,128,128]{2,1,0:T(8,128)}, f32[3,128,128]{2,1,0:T(8,128)}, f32[128,128]{1,0:T(8,128)}, f32[128,128]{1,0:T(8,128)}) custom-call(f32[320,128]{1,0:T(8,128)} %shard_map.103.pooled, f32[3,128,128]{2,1,0:T(8,128)} %w_query.5, f32[3,128,128]{2,1,0:T(8,128)} %w_key.5, f32[896,128]{1,0:T(8,128)} %shard_map.110.total), custom_call_target="tpu_custom_call" | custom-call | tf_op jit(solution)/shard_map/pallas_call | solution.py:383
  191.6 4.4 %shard_map.112 = bf16[64,128,128]{2,1,0:T(8,128)(2,1)} custom-call(bf16[64,128,128]{2,1,0:T(8,128)(2,1)} %get-tuple-element.33.grad_values, bf16[128,128]{1,0:T(8,128)(2,1)} %w_value.5, f32[320,128]{1,0:T(8,128)} %get-tuple-element.48.means_grad), custom_call_target="tpu_custom_call" | custom-call | tf_op jit(solution)/shard_map/pallas_call | solution.py:184
Async XLA Ops:
  4.6 62.4 %all-to-all-start = ((bf16[128,64,128]{2,1,0:T(8,128)(2,1)}), bf16[128,64,128]{2,1,0:T(8,128)(2,1)S(1)}, u32[]{:S(2)}, u32[]{:S(2)}) async-start(bf16[128,64,128]{2,1,0:T(8,128)(2,1)} %shard_map.101), calls=%async_computation | async-start | bytes 4194304 | tf_op jit(solution)/shard_map/all_to_all | solution.py:466
  67.0 7.2 %copy-start.1 = (bf16[128,64,128]{2,1,0:T(8,128)(2,1)}, bf16[128,64,128]{2,1,0:T(8,128)(2,1)S(1)}, u32[]{:S(2)}) copy-start(bf16[128,64,128]{2,1,0:T(8,128)(2,1)S(1)} %all-to-all-done) | copy-start | bytes 6291460
  67.0 36.8 %all-to-all-start.2 = ((bf16[128,64,128]{2,1,0:T(8,128)(2,1)}), bf16[128,64,128]{2,1,0:T(8,128)(2,1)}, u32[]{:S(2)}, u32[]{:S(2)}) async-start(bf16[128,64,128]{2,1,0:T(8,128)(2,1)} %shard_map.107), calls=%async_computation.2 | async-start | bytes 4194304 | tf_op jit(solution)/shard_map/all_to_all | solution.py:466
  103.8 34.8 %all-to-all-start.1 = ((bf16[128,64,128]{2,1,0:T(8,128)(2,1)}), bf16[128,64,128]{2,1,0:T(8,128)(2,1)S(1)}, u32[]{:S(2)}, u32[]{:S(2)}) async-start(bf16[128,64,128]{2,1,0:T(8,128)(2,1)} %bitcast.11), calls=%async_computation.1 | async-start | bytes 4194304 | tf_op jit(solution)/shard_map/all_to_all | solution.py:466
  138.6 1.3 copy-start

commit v2 on v0

v2 whole, which is shorter than its diff:
```python
import jax
import jax.numpy as jnp
from jax import lax
from jax.experimental import pallas as pl
from jax.experimental.pallas import tpu as pltpu
from jax.sharding import PartitionSpec as P

BF = jnp.bfloat16
F32 = jnp.float32
MESH = pl.DeviceIdType.MESH
H = 8
D = 16
C = 128
Z, Y, X = 64, 128, 128
ZL, YL = 2, 32
CELLS = ZL * YL
GZ, GY = 32, 4
EPS = 1e-06
HIGH = lax.Precision.HIGHEST
COUNTS = (Y * X, Z * X, Z * Y)
STARTS = (0, Z, Z + Y)
LENGTHS = (Z, Y, X)
POOLED = Z + Y + X
VMEM = pl.BlockSpec(memory_space=pltpu.VMEM)


def params(**more):
    return pltpu.CompilerParams(vmem_limit_bytes=56 * 2**20, **more)


def dot(a, b):
    return jnp.dot(a, b, preferred_element_type=F32)


def dot_nt(a, b, precision=None):
    return lax.dot_general(
        a, b, (((1,), (1,)), ((), ())), preferred_element_type=F32, precision=precision
    )


def dot_tn(a, b, precision=None):
    return lax.dot_general(
        a, b, (((0,), (0,)), ((), ())), preferred_element_type=F32, precision=precision
    )


def head_stack(block):
    head = lax.broadcasted_iota(jnp.int32, block.shape, 1) % C // D
    zero = jnp.zeros((), block.dtype)
    return jnp.concatenate([jnp.where(head == h, block, zero) for h in range(H)], axis=0)


def pair_lanes(first, second):
    return jnp.concatenate([first, second], axis=1)


def normalise(pooled, axis):
    means = pooled[pl.ds(STARTS[axis], LENGTHS[axis]), :] / COUNTS[axis]
    scale = lax.rsqrt(jnp.mean(means * means, axis=-1, keepdims=True) + EPS)
    return means * scale, scale


def project(normed, weight):
    return jnp.dot(normed, weight, preferred_element_type=F32, precision=HIGH)


def attention(pooled, w_query, w_key, axis, attn, kernel, back):
    length = LENGTHS[axis]
    normed, _ = normalise(pooled, axis)
    queries = project(normed, w_query[axis])
    keys = project(normed, w_key[axis])
    scores = dot_nt(head_stack(queries), keys, HIGH) * (1.0 / D**0.5)
    grown = jnp.exp(scores - jnp.max(scores, axis=-1, keepdims=True))
    soft = grown / jnp.sum(grown, axis=-1, keepdims=True)
    attn[...] = soft
    heads = [soft[h * length : (h + 1) * length] for h in range(H)]
    kernel[...] = jnp.concatenate(heads, axis=1).astype(BF)
    back[...] = jnp.concatenate([head.T for head in heads], axis=1).astype(BF)


def pull(pooled, w_query, w_key, axis, attn, score, out, row_q, row_k):
    length = LENGTHS[axis]
    normed, _ = normalise(pooled, axis)
    queries = head_stack(project(normed, w_query[axis]))
    keys = head_stack(project(normed, w_key[axis]))
    soft, grad = attn[...], score[...]
    inner = jnp.sum(soft * grad, axis=-1, keepdims=True)
    grad = soft * (grad - inner) * (1.0 / D**0.5)
    heads = [grad[h * length : (h + 1) * length] for h in range(H)]
    out[pl.ds(row_q, length), :] = jnp.dot(
        jnp.concatenate(heads, axis=1), keys, preferred_element_type=F32, precision=HIGH
    )
    out[pl.ds(row_k, length), :] = dot_tn(grad, queries, HIGH)


def settle(pooled, w_query, w_key, axis, total, row_q, row_k, query_grad, key_grad):
    length = LENGTHS[axis]
    normed, scale = normalise(pooled, axis)
    grad_q = total[pl.ds(row_q, length), :]
    grad_k = total[pl.ds(row_k, length), :]
    query_grad[axis] = dot_tn(normed, grad_q, HIGH)
    key_grad[axis] = dot_tn(normed, grad_k, HIGH)
    grad = dot_nt(grad_q, w_query[axis], HIGH) + dot_nt(grad_k, w_key[axis], HIGH)
    inner = jnp.mean(grad * normed, axis=-1, keepdims=True)
    return scale * (grad - normed * inner) / COUNTS[axis]


def place():
    gz, gy = lax.axis_index("gz"), lax.axis_index("gy")
    return gz // 8, (gz // 2) % 4, (gy // 2) * 2 + gz % 2, gy % 2


def shifted(step):
    z, y, x, core = place()
    k = (step * 37) % 128
    to_core = (core + k) % 2
    to_x = (x + (k // 2)) % 4
    to_y = (y + (k // 8)) % 4
    to_z = (z + (k // 32)) % 4
    return (to_z * 4 + to_y) * 2 + to_x % 2, (to_x // 2) * 2 + to_core


def mine():
    return lax.axis_index("gz") * GY + lax.axis_index("gy")


def wait_bytes(ref, sem):
    pltpu.make_async_copy(ref, ref, sem).wait()


def send_all(src, dst, send_sem, recv_sem):
    me = mine()

    def send(step, carry):
        gz, gy = shifted(step)
        pltpu.make_async_remote_copy(
            src.at[gz * GY + gy], dst.at[me], send_sem, recv_sem, device_id=(gz, gy), device_id_type=MESH
        ).start()
        return carry

    lax.fori_loop(1, 128, send, 0)
    dst[me] = src[me]


def wait_all(ref, sem):
    wait_bytes(ref.at[pl.ds(0, 127)], sem)


class Sum:
    def __init__(self, src, out, near, wide, sems):
        self.src, self.out, self.near, self.wide, self.sems = src, out, near, wide, sems
        self.piece = src.shape[0] // 8
        gz, gy = lax.axis_index("gz"), lax.axis_index("gy")
        self.gz, self.gy = gz, gy
        self.line, self.side = gz // 2, (gz % 2) * 4 + gy

    def rows(self, index):
        return pl.ds(pl.multiple_of(index * self.piece, 8), self.piece)

    def near_peer(self, k):
        peer = (self.side + k) % 8
        return peer, (self.line * 2 + peer // 4, peer % 4)

    def wide_peer(self, k):
        peer = (self.line + k) % 16
        return peer, (peer * 2 + self.gz % 2, self.gy)

    def copy(self, src, dst, first, device):
        pltpu.make_async_remote_copy(
            src, dst, self.sems.at[first], self.sems.at[first + 1], device_id=device, device_id_type=MESH
        ).start()

    def first(self):
        for k in range(1, 8):
            peer, device = self.near_peer(k)
            self.copy(self.src.at[self.rows(peer)], self.near.at[self.side], 0, device)
        self.near[self.side] = self.src[self.rows(self.side)]

    def second(self):
        wait_bytes(self.near.at[pl.ds(0, 7)], self.sems.at[1])
        self.wide[self.line] = jnp.sum(self.near[...], axis=0)
        for k in range(1, 16):
            peer, device = self.wide_peer(k)
            self.copy(self.wide.at[self.line], self.wide.at[self.line], 2, device)

    def third(self):
        wait_bytes(self.wide.at[pl.ds(0, 15)], self.sems.at[3])
        rows = self.rows(self.side)
        self.out[rows] = jnp.sum(self.wide[...], axis=0)
        for k in range(1, 8):
            peer, device = self.near_peer(k)
            self.copy(self.out.at[rows], self.out.at[rows], 4, device)

    def end(self):
        wait_bytes(self.near.at[pl.ds(0, 7)], self.sems.at[5])

    def close(self):
        wait_bytes(self.near.at[pl.ds(0, 7)], self.sems.at[0])
        wait_bytes(self.wide.at[pl.ds(0, 15)], self.sems.at[2])
        wait_bytes(self.near.at[pl.ds(0, 7)], self.sems.at[4])


def whole_kernel(
    fields_in, cot_in, w_value, w_out, w_query, w_key,
    field_grad, value_grad, out_grad, query_grad, key_grad,
    fields, cot, cot_s, cot_r, cot_y, mixed_y, grad_y, grad_s, after_s, after_r, after_y, grad_r, values, grad_values, direct,
    held,
    attn_z, kernel_z, back_z, attn_y, kernel_y, back_y, attn_x, kernel_x, back_x,
    score_z, score_y, score_x, value_part,
    sum0, pooled, near0, wide0, sum1, total1, near1, wide1, sum2, total2, near2, wide2,
    load_sems, store_sems, move_sems, sums0, sums1, sums2,
):
    gz, gy = lax.axis_index("gz"), lax.axis_index("gy")

    def load(i, src, dst, base):
        return pltpu.make_async_copy(src.at[pl.ds(16 * i, 16)], dst.at[pl.ds(16 * i, 16)], load_sems.at[base + i])

    for i in range(4):
        load(i, fields_in, fields, 0).start()
    for i in range(4):
        load(i, cot_in, cot, 4).start()

    barrier = pltpu.get_barrier_semaphore()

    def greet(step, carry):
        pl.semaphore_signal(barrier, inc=1, device_id=shifted(step), device_id_type=MESH)
        return carry

    lax.fori_loop(1, 128, greet, 0)

    sum0[...] = jnp.zeros_like(sum0)
    for i in range(4):
        load(i, fields_in, fields, 0).wait()
        block = fields[pl.ds(16 * i, 16)].astype(F32)
        cells = jnp.sum(block, axis=1)
        sum0[pl.ds(Z + Y, X), :] += jnp.sum(block, axis=0)
        sum0[pl.ds(gz * ZL + i // 2, 1), :] += jnp.sum(cells, axis=0, keepdims=True)
        sum0[pl.ds(pl.multiple_of(Z + gy * YL + (i % 2) * 16, 16), 16), :] += cells
    means = Sum(sum0, pooled, near0, wide0, sums0)
    pl.semaphore_wait(barrier, 127)
    means.first()
    for i in range(4):
        load(i, cot_in, cot, 4).wait()
        cot_s[:, pl.ds(16 * i, 16), :] = jnp.swapaxes(cot[pl.ds(16 * i, 16)], 0, 1)
    means.second()
    for i in range(4):
        flat = fields[pl.ds(16 * i, 16)].reshape(16 * X, C)
        values[pl.ds(16 * i, 16)] = dot(flat, w_value[...]).astype(BF).reshape(16, X, C)
    means.third()
    send_all(cot_s, cot_r, move_sems.at[0], move_sems.at[1])
    means.end()

    attention(pooled, w_query, w_key, 2, attn_x, kernel_x, back_x)
    means.close()

    def over_x(i, carry):
        start = pl.multiple_of(i * 16, 16)
        for t in range(0, 16, 2):
            wide = head_stack(pair_lanes(values[start + t], values[start + t + 1]))
            done = dot(kernel_x[...], wide).astype(BF)
            held[t] = done[:, :C]
            held[t + 1] = done[:, C:]
        after_s[:, pl.ds(start, 16), :] = jnp.swapaxes(held[...], 0, 1)
        return carry

    lax.fori_loop(0, 4, over_x, 0)
    send_all(after_s, after_r, move_sems.at[2], move_sems.at[3])
    attention(pooled, w_query, w_key, 0, attn_z, kernel_z, back_z)
    attention(pooled, w_query, w_key, 1, attn_y, kernel_y, back_y)

    wait_all(cot_r, move_sems.at[1])

    def back_over_z(step, carry):
        side, start = step // 2, pl.multiple_of((step % 2) * 16, 16)
        y_start = pl.multiple_of(step * 16, 16)
        lines = []
        for low in range(ZL):
            lines.append(
                jnp.stack(
                    [cot_r[g * GY + side, pl.ds(low * YL + start, 16), :] for g in range(GZ)], axis=0
                )
            )
        block = jnp.stack(lines, axis=1).reshape(Z, 16, C)
        turned = jnp.swapaxes(block, 0, 1)
        cot_y[pl.ds(y_start, 16)] = turned
        grad_mixed = dot_nt(turned.reshape(16 * Z, C), w_out[...]).astype(BF).reshape(16, Z, C)
        mixed_y[pl.ds(y_start, 16)] = grad_mixed
        for t in range(0, 16, 2):
            wide = head_stack(pair_lanes(grad_mixed[t], grad_mixed[t + 1]))
            done = dot(back_z[...], wide).astype(BF)
            held[t, pl.ds(0, Z), :] = done[:, :C]
            held[t + 1, pl.ds(0, Z), :] = done[:, C:]
        grad_y[:, pl.ds(y_start, 16), :] = jnp.swapaxes(held[:, pl.ds(0, Z), :], 0, 1)
        return carry

    lax.fori_loop(0, 8, back_over_z, 0)

    def back_over_y(t, carry):
        wide = head_stack(pair_lanes(grad_y[2 * t], grad_y[2 * t + 1]))
        done = dot(back_y[...], wide).astype(BF)
        for side in range(GY):
            for low in range(ZL):
                grad_s[t * GY + side, pl.ds(low * YL, YL), :] = done[
                    side * YL : (side + 1) * YL, low * C : (low + 1) * C
                ]
        return carry

    lax.fori_loop(0, Z // 2, back_over_y, 0)
    send_all(grad_s, grad_r, move_sems.at[4], move_sems.at[5])

    score_z[...] = jnp.zeros_like(score_z)
    score_y[...] = jnp.zeros_like(score_y)
    sum1[pl.ds(2 * (Z + Y), C), :] = jnp.zeros((C, C), F32)
    wait_all(after_r, move_sems.at[3])

    def over_y(t, carry):
        lines = []
        for low in range(ZL):
            lines.append(
                jnp.concatenate([after_r[t * GY + side, pl.ds(low * YL, YL), :] for side in range(GY)], axis=0)
            )
        block = pair_lanes(lines[0], lines[1])
        done = dot(kernel_y[...], head_stack(block)).astype(BF)
        after_y[2 * t] = done[:, :C]
        after_y[2 * t + 1] = done[:, C:]
        score_y[...] += dot_nt(head_stack(pair_lanes(grad_y[2 * t], grad_y[2 * t + 1])), block)
        return carry

    lax.fori_loop(0, Z // 2, over_y, 0)

    def over_z(step, carry):
        y_start = pl.multiple_of(step * 16, 16)
        lines = jnp.swapaxes(after_y[:, pl.ds(y_start, 16), :], 0, 1)
        grad_mixed = mixed_y[pl.ds(y_start, 16)]
        parts = []
        total = jnp.zeros((H * Z, Z), F32)
        for t in range(0, 16, 2):
            block = pair_lanes(lines[t], lines[t + 1])
            done = dot(kernel_z[...], head_stack(block)).astype(BF)
            parts += [done[:, :C], done[:, C:]]
            total += dot_nt(head_stack(pair_lanes(grad_mixed[t], grad_mixed[t + 1])), block)
        score_z[...] += total
        mixed = jnp.concatenate(parts, axis=0)
        sum1[pl.ds(2 * (Z + Y), C), :] += dot_tn(mixed, cot_y[pl.ds(y_start, 16)].reshape(16 * Z, C))
        return carry

    lax.fori_loop(0, 8, over_z, 0)
    pull(pooled, w_query, w_key, 0, attn_z, score_z, sum1, 0, Z)
    pull(pooled, w_query, w_key, 1, attn_y, score_y, sum1, 2 * Z, 2 * Z + Y)
    early = Sum(sum1, total1, near1, wide1, sums1)
    early.first()

    score_x[...] = jnp.zeros_like(score_x)
    value_part[...] = jnp.zeros_like(value_part)
    wait_all(grad_r, move_sems.at[5])

    def home(i, carry):
        start = pl.multiple_of(i * 16, 16)
        grad_x = jnp.swapaxes(grad_r[:, pl.ds(start, 16), :], 0, 1)
        total = jnp.zeros((H * X, X), F32)
        for t in range(0, 16, 2):
            wide = head_stack(pair_lanes(grad_x[t], grad_x[t + 1]))
            done = dot(back_x[...], wide).astype(BF)
            grad_values[start + t] = done[:, :C]
            grad_values[start + t + 1] = done[:, C:]
            total += dot_nt(wide, pair_lanes(values[start + t], values[start + t + 1]))
        score_x[...] += total
        grad = grad_values[pl.ds(start, 16)].reshape(16 * X, C)
        value_part[...] += dot_tn(fields[pl.ds(start, 16)].reshape(16 * X, C), grad)
        return carry

    lax.fori_loop(0, 2, home, 0)
    early.second()
    lax.fori_loop(2, 4, home, 0)
    early.third()
    pull(pooled, w_query, w_key, 2, attn_x, score_x, sum2, 0, X)
    sum2[pl.ds(2 * X, C), :] = value_part[...]
    late = Sum(sum2, total2, near2, wide2, sums2)
    late.first()
    early.end()
    means_z = settle(pooled, w_query, w_key, 0, total1, 0, Z, query_grad, key_grad)
    late.second()
    means_y = settle(pooled, w_query, w_key, 1, total1, 2 * Z, 2 * Z + Y, query_grad, key_grad)
    out_grad[...] = total1[pl.ds(2 * (Z + Y), C), :]
    sum0[pl.ds(0, Z), :] = means_z
    sum0[pl.ds(Z, Y), :] = means_y
    late.third()

    def project_back(i, carry):
        start = pl.multiple_of(i * 16, 16)
        grad = grad_values[pl.ds(start, 16)].reshape(16 * X, C)
        direct[pl.ds(start, 16)] = dot_nt(grad, w_value[...]).reshape(16, X, C)
        return carry

    lax.fori_loop(0, 4, project_back, 0)
    late.end()
    means_x = settle(pooled, w_query, w_key, 2, total2, 0, X, query_grad, key_grad)
    value_grad[...] = total2[pl.ds(2 * X, C), :]

    def store(i):
        return pltpu.make_async_copy(grad_values.at[pl.ds(16 * i, 16)], field_grad.at[pl.ds(16 * i, 16)], store_sems.at[i])

    for i in range(4):
        part_z = sum0[pl.ds(gz * ZL + i // 2, 1), :]
        part_y = sum0[pl.ds(pl.multiple_of(Z + gy * YL + (i % 2) * 16, 16), 16), :]
        cells = part_z + part_y
        grad_values[pl.ds(16 * i, 16)] = (direct[pl.ds(16 * i, 16)] + cells[:, None, :] + means_x[None]).astype(BF)
        store(i).start()
    for i in range(4):
        store(i).wait()
    wait_all(cot_s, move_sems.at[0])
    wait_all(after_s, move_sems.at[2])
    wait_all(grad_s, move_sems.at[4])
    early.close()
    late.close()


def local(fields, cotangent, w_value, w_out, w_query, w_key):
    any_space = pl.BlockSpec(memory_space=pl.ANY)
    cells = (CELLS, X, C)
    blocks = (X, CELLS, C)
    sums = []
    for rows in (POOLED, 2 * (Z + Y) + C, 2 * X + C):
        sums += [
            pltpu.VMEM((rows, C), F32),
            pltpu.VMEM((rows, C), F32),
            pltpu.VMEM((8, rows // 8, C), F32),
            pltpu.VMEM((16, rows // 8, C), F32),
        ]
    map_shapes = []
    for length in LENGTHS:
        map_shapes += [
            pltpu.VMEM((H * length, length), F32),
            pltpu.VMEM((length, H * length), BF),
            pltpu.VMEM((length, H * length), BF),
        ]
    field_shapes = [
        cells, cells, blocks, blocks, (Y, Z, C), (Y, Z, C), (Z, Y, C), blocks, blocks, blocks, (Z, Y, C), blocks,
        cells, cells,
    ]
    square = jax.ShapeDtypeStruct((C, C), F32)
    cube = jax.ShapeDtypeStruct((3, C, C), F32)
    field_grad, value_grad, out_grad, query_grad, key_grad = pl.pallas_call(
        whole_kernel,
        in_specs=[any_space] * 2 + [VMEM] * 4,
        out_specs=[any_space] + [VMEM] * 4,
        out_shape=[jax.ShapeDtypeStruct(cells, BF), square, square, cube, cube],
        scratch_shapes=[pltpu.VMEM(shape, BF) for shape in field_shapes]
        + [pltpu.VMEM(cells, F32), pltpu.VMEM((16, X, C), BF)]
        + map_shapes
        + [
            pltpu.VMEM((H * Z, Z), F32),
            pltpu.VMEM((H * Y, Y), F32),
            pltpu.VMEM((H * X, X), F32),
            pltpu.VMEM((C, C), F32),
        ]
        + sums
        + [pltpu.SemaphoreType.DMA((count,)) for count in (8, 4, 6, 6, 6, 6)],
        compiler_params=params(collective_id=0, has_side_effects=True),
    )(fields.reshape(cells), cotangent.reshape(cells), w_value, w_out, w_query, w_key)
    return (field_grad.reshape(ZL, YL, X, C), value_grad, out_grad, query_grad, key_grad)


def solution(mesh):
    placed = (P("gz", "gy", None, None), P("gz", "gy", None, None), P(), P(), P(), P())
    return jax.shard_map(
        local,
        mesh=mesh,
        in_specs=placed,
        out_specs=(P("gz", "gy", None, None), P(), P(), P(), P()),
        check_vma=False,
    )
```

time: 736 us -> 146 us (0.20); the launches traced: 724 us -> 146 us
  waiting for transfers between devices: 311 us -> 0 us
  local copies, waits for them, and re-layouts: 205 us -> 5.84 us
  Pallas kernels: 0 us -> 139 us
  blocking collectives: 81.3 us -> 0 us
  matrix products: 64.6 us -> 0 us
  starting transfers between devices: 36.6 us -> 0 us
  between operations: 15.2 us -> 0.68 us
  other arithmetic: 10.5 us -> 0 us
    psum x2 -> x0, waiting for transfers between devices: 283 us -> none  [the longest x1 144 us: local(): lax.psum((score_x_part, value_part, out_part), ('gz', 'gy'))]
    pallas_call x0 -> x1, Pallas kernels: none -> 139 us  [local(): pl.pallas_call(whole_kernel, in_specs=[any_space] * 2 + [VMEM] * 4, out_s...]
    psum x1 -> x0, blocking collectives: 81.3 us -> none  [local(): lax.psum((placed_z, placed_y, sum_x), ('gz', 'gy'))]
    dot_general x41 -> x0, matrix products: 64.6 us -> none  [the longest x6 26.8 us: contract(): jnp.einsum(pattern, matrix, head_view(field), preferred_element_type=jnp....]
    reshape x8 -> x0, local copies, waits for them, and re-layouts: 63 us -> none  [the longest x4 43.7 us: head_view(): return field.reshape(field_shape[:3] + (H, field_shape[3] // H))]
    all_to_all x7 -> x0, local copies, waits for them, and re-layouts: 45.3 us -> none  [the longest x1 11.3 us: local(): lax.all_to_all(after_x, 'gy', split_axis=2, concat_axis=1, tiled=True)]
    convert_element_type x9 -> x0, local copies, waits for them, and re-layouts: 42.7 us -> none  [the longest x7 34.5 us: contract(): return result.astype(jnp.bfloat16).reshape(field.shape)]
    another operation x4 -> x0, local copies, waits for them, and re-layouts: 38.2 us -> none  [the longest x2 22.2 us: head_view(): return field.reshape(field_shape[:3] + (H, field_shape[3] // H))]
  transfers between devices with their start and end apart: 8 -> 0, of which waited for: 4 -> 0; matrix products, arithmetic and copies ran while one was open for 26% -> 0% of each run, Pallas kernels for 0% -> 0%
where the time goes in v2:
time: 146 us
  Pallas kernels  139 us (95%)
  local copies, waits for them, and re-layouts  5.84 us (4%)
    pallas_call x1, Pallas kernels, local(): pl.pallas_call(whole_kernel, in_specs=[any_space] * 2 + [VMEM] * 4, out_s...  139 us
    unnamed x13, local copies, waits for them, and re-layouts  5.84 us

profile of v2, /device:TPU:1, one launch (start us, length us, event | category | flops | bytes accessed | tf_op | source)
XLA Modules:
  0.0 145.7 jit_solution(6882347065100486993)
XLA Ops:
  0.6 139.1 %shard_map.101 = (bf16[64,128,128]{2,1,0:T(8,128)(2,1)}, f32[128,128]{1,0:T(8,128)}, f32[128,128]{1,0:T(8,128)}, f32[3,128,128]{2,1,0:T(8,128)}, f32[3,128,128]{2,1,0:T(8,128)}) custom-call(bf16[64,128,128]{2,1,0:T(8,128)(2,1)} %bitcast.3, bf16[64,128,128]{2,1,0:T(8,128)(2,1)} %bitcast.4, bf16[128,128]{1,0:T(8,128)(2,1)} %w_value.1, bf16[128,128]{1,0:T(8,128)(2,1)} %w_out.1, ...), custom_call_target="tpu_custom_call" | custom-call | tf_op jit(solution)/shard_map/pallas_call | solution.py:443
  139.8 0.0 copy-start.3
  139.8 0.0 copy-start.2
  139.8 0.0 copy-start.1
  139.8 0.0 copy-start
  139.8 3.2 %copy.16 = bf16[2,32,128,128]{3,2,1,0:T(8,128)(2,1)} copy(bf16[2,32,128,128]{3,2,1,0:T(8,128)(2,1)} %bitcast.5) | data formatting | bytes 4194304
  143.0 0.0 copy-done.3
  143.0 0.6 copy.17
  143.7 0.0 copy-done.2
  143.7 0.6 copy.18
  144.3 0.0 copy-done.1
  144.3 0.7 copy.19
  145.0 0.0 copy-done
  145.0 0.7 copy.20
Async XLA Ops:
  139.8 3.3 %copy-start.3 = (f32[128,128]{1,0:T(8,128)S(1)}, f32[128,128]{1,0:T(8,128)}, u32[]{:S(2)}) copy-start(f32[128,128]{1,0:T(8,128)} %get-tuple-element.21) | copy-start | bytes 196612
  139.8 3.9 %copy-start.2 = (f32[128,128]{1,0:T(8,128)S(1)}, f32[128,128]{1,0:T(8,128)}, u32[]{:S(2)}) copy-start(f32[128,128]{1,0:T(8,128)} %get-tuple-element.22) | copy-start | bytes 196612
  139.8 4.5 %copy-start.1 = (f32[3,128,128]{2,1,0:T(8,128)S(1)}, f32[3,128,128]{2,1,0:T(8,128)}, u32[]{:S(2)}) copy-start(f32[3,128,128]{2,1,0:T(8,128)} %get-tuple-element.23) | copy-start | bytes 589828
  139.8 5.2 %copy-start = (f32[3,128,128]{2,1,0:T(8,128)S(1)}, f32[3,128,128]{2,1,0:T(8,128)}, u32[]{:S(2)}) copy-start(f32[3,128,128]{2,1,0:T(8,128)} %get-tuple-element.24) | copy-start | bytes 589828

commit v3 on v2

v3 whole, which is shorter than its diff:
```python
import jax
import jax.numpy as jnp
from jax import lax
from jax.experimental import pallas as pl
from jax.experimental.pallas import tpu as pltpu
from jax.sharding import PartitionSpec as P

BF = jnp.bfloat16
F32 = jnp.float32
MESH = pl.DeviceIdType.MESH
H = 8
D = 16
C = 128
Z, Y, X = 64, 128, 128
ZL, YL = 2, 32
CELLS = ZL * YL
GZ, GY = 32, 4
EPS = 1e-06
HIGH = lax.Precision.HIGHEST
COUNTS = (Y * X, Z * X, Z * Y)
STARTS = (0, Z, Z + Y)
LENGTHS = (Z, Y, X)
POOLED = Z + Y + X
VMEM = pl.BlockSpec(memory_space=pltpu.VMEM)


def params(**more):
    return pltpu.CompilerParams(vmem_limit_bytes=56 * 2**20, **more)


def dot(a, b):
    return jnp.dot(a, b, preferred_element_type=F32)


def dot_nt(a, b, precision=None):
    return lax.dot_general(
        a, b, (((1,), (1,)), ((), ())), preferred_element_type=F32, precision=precision
    )


def dot_tn(a, b, precision=None):
    return lax.dot_general(
        a, b, (((0,), (0,)), ((), ())), preferred_element_type=F32, precision=precision
    )


def head_stack(block):
    head = lax.broadcasted_iota(jnp.int32, block.shape, 1) % C // D
    zero = jnp.zeros((), block.dtype)
    return jnp.concatenate([jnp.where(head == h, block, zero) for h in range(H)], axis=0)


def mix(kernel, lines):
    done = dot(kernel[...], head_stack(jnp.concatenate(lines, axis=1))).astype(BF)
    return [done[:, C * t : C * (t + 1)] for t in range(len(lines))]


def pair_up(left, right):
    return dot_nt(head_stack(jnp.concatenate(left, axis=1)), jnp.concatenate(right, axis=1))


def normalise(pooled, axis):
    means = pooled[pl.ds(STARTS[axis], LENGTHS[axis]), :] / COUNTS[axis]
    scale = lax.rsqrt(jnp.mean(means * means, axis=-1, keepdims=True) + EPS)
    return means * scale, scale


def project(normed, weight):
    return jnp.dot(normed, weight, preferred_element_type=F32, precision=HIGH)


def attention(pooled, w_query, w_key, axis, attn, kernel, back):
    length = LENGTHS[axis]
    normed, _ = normalise(pooled, axis)
    queries = project(normed, w_query[axis])
    keys = project(normed, w_key[axis])
    scores = dot_nt(head_stack(queries), keys, HIGH) * (1.0 / D**0.5)
    grown = jnp.exp(scores - jnp.max(scores, axis=-1, keepdims=True))
    soft = grown / jnp.sum(grown, axis=-1, keepdims=True)
    attn[...] = soft
    heads = [soft[h * length : (h + 1) * length] for h in range(H)]
    kernel[...] = jnp.concatenate(heads, axis=1).astype(BF)
    back[...] = jnp.concatenate([head.T for head in heads], axis=1).astype(BF)


def pull(pooled, w_query, w_key, axis, attn, score, out, row_q, row_k):
    length = LENGTHS[axis]
    normed, _ = normalise(pooled, axis)
    queries = head_stack(project(normed, w_query[axis]))
    keys = head_stack(project(normed, w_key[axis]))
    soft, grad = attn[...], score[...]
    inner = jnp.sum(soft * grad, axis=-1, keepdims=True)
    grad = soft * (grad - inner) * (1.0 / D**0.5)
    heads = [grad[h * length : (h + 1) * length] for h in range(H)]
    out[pl.ds(row_q, length), :] = jnp.dot(
        jnp.concatenate(heads, axis=1), keys, preferred_element_type=F32, precision=HIGH
    )
    out[pl.ds(row_k, length), :] = dot_tn(grad, queries, HIGH)


def settle(pooled, w_query, w_key, axis, total, row_q, row_k, out, out_q, out_k):
    length = LENGTHS[axis]
    normed, scale = normalise(pooled, axis)
    grad_q = total[pl.ds(row_q, length), :]
    grad_k = total[pl.ds(row_k, length), :]
    out[pl.ds(out_q, C), :] = dot_tn(normed, grad_q, HIGH)
    out[pl.ds(out_k, C), :] = dot_tn(normed, grad_k, HIGH)
    grad = dot_nt(grad_q, w_query[axis], HIGH) + dot_nt(grad_k, w_key[axis], HIGH)
    inner = jnp.mean(grad * normed, axis=-1, keepdims=True)
    return scale * (grad - normed * inner) / COUNTS[axis]


def torus():
    gz, gy = lax.axis_index("gz"), lax.axis_index("gy")
    z, y = lax.div(gz, 8), lax.rem(lax.div(gz, 2), 4)
    x, core = lax.div(gy, 2) * 2 + lax.rem(gz, 2), lax.rem(gy, 2)
    lines = [
        [(lax.rem(z + dz, 4) * 4 + lax.rem(y + dy, 4)) * 2 for dy in range(4)] for dz in range(4)
    ]
    return lines, x, core


def shifts(step, first=0):
    lines, x, core = torus()
    to_core = lax.rem(core + lax.rem(step, 2), 2)
    turn = x + lax.div(step, 2)
    sides = []
    for dx in range(4):
        to_x = lax.rem(turn + dx, 4)
        sides.append((lax.rem(to_x, 2), lax.div(to_x, 2) * 2 + to_core))
    found = []
    for j in range(first, 16):
        dz, dy = j % 4, (j // 4 + j) % 4
        low, gy = sides[(j // 4 + 2 * j) % 4]
        found.append((lines[dz][dy] + low, gy))
    return found


def each_device(visit, first, last):
    def step(i, carry):
        for device in shifts(i):
            visit(device)
        return carry

    if first == 0:
        for device in shifts(jnp.int32(0), 1):
            visit(device)
        first = 1
    lax.fori_loop(first, last, step, 0)


def mine():
    return lax.axis_index("gz") * GY + lax.axis_index("gy")


def wait_bytes(ref, sem):
    pltpu.make_async_copy(ref, ref, sem).wait()


def send(src, dst, send_sem, recv_sem, first=0, last=8, part=None):
    me = mine()

    def block(ref, index):
        return ref.at[index] if part is None else ref.at[index, part]

    def visit(device):
        pltpu.make_async_remote_copy(
            block(src, device[0] * GY + device[1]), block(dst, me), send_sem, recv_sem,
            device_id=device, device_id_type=MESH,
        ).start()

    each_device(visit, first, last)


def keep(src, dst):
    me = mine()
    dst[me] = src[me]


def wait_all(ref, sem, part=None):
    if part is None:
        wait_bytes(ref.at[pl.ds(0, 127)], sem)
    else:
        wait_bytes(ref.at[pl.ds(0, 127), part], sem)


class Sum:
    def __init__(self, src, out, near, wide, sems):
        self.src, self.out, self.near, self.wide, self.sems = src, out, near, wide, sems
        self.piece = src.shape[0] // 8
        gz, gy = lax.axis_index("gz"), lax.axis_index("gy")
        self.gz, self.gy = gz, gy
        self.line, self.side = lax.div(gz, 2), lax.rem(gz, 2) * 4 + gy

    def rows(self, index):
        return pl.ds(pl.multiple_of(index * self.piece, 8), self.piece)

    def near_peer(self, k):
        peer = lax.rem(self.side + k, 8)
        return peer, (self.line * 2 + lax.div(peer, 4), lax.rem(peer, 4))

    def wide_peer(self, k):
        peer = lax.rem(self.line + k, 16)
        return peer, (peer * 2 + lax.rem(self.gz, 2), self.gy)

    def copy(self, src, dst, first, device):
        pltpu.make_async_remote_copy(
            src, dst, self.sems.at[first], self.sems.at[first + 1], device_id=device, device_id_type=MESH
        ).start()

    def first(self):
        for k in range(1, 8):
            peer, device = self.near_peer(k)
            self.copy(self.src.at[self.rows(peer)], self.near.at[self.side], 0, device)
        self.near[self.side] = self.src[self.rows(self.side)]

    def second(self):
        wait_bytes(self.near.at[pl.ds(0, 7)], self.sems.at[1])
        self.wide[self.line] = jnp.sum(self.near[...], axis=0)
        for k in range(1, 16):
            peer, device = self.wide_peer(k)
            self.copy(self.wide.at[self.line], self.wide.at[self.line], 2, device)

    def third(self):
        wait_bytes(self.wide.at[pl.ds(0, 15)], self.sems.at[3])
        rows = self.rows(self.side)
        self.out[rows] = jnp.sum(self.wide[...], axis=0)
        for k in range(1, 8):
            peer, device = self.near_peer(k)
            self.copy(self.out.at[rows], self.out.at[rows], 4, device)

    def end(self):
        wait_bytes(self.near.at[pl.ds(0, 7)], self.sems.at[5])

    def close(self):
        wait_bytes(self.near.at[pl.ds(0, 7)], self.sems.at[0])
        wait_bytes(self.wide.at[pl.ds(0, 15)], self.sems.at[2])
        wait_bytes(self.near.at[pl.ds(0, 7)], self.sems.at[4])


def whole_kernel(
    fields_in, cot_in, w_value_in, w_out_in, w_query_in, w_key_in,
    grad_values_out, rest_out,
    fields, cot, cot_s, cot_r, cot_y, mixed_y, grad_y, grad_s, after_s, after_r, after_y, grad_r, values, grad_values,
    held, w_value, w_out, w_query, w_key,
    attn_z, kernel_z, back_z, attn_y, kernel_y, back_y, attn_x, kernel_x, back_x,
    score_z, score_y, score_x, early_rest,
    sum0, pooled, near0, wide0, sum1, total1, near1, wide1, sum2, total2, near2, wide2,
    load_sems, store_sems, move_sems, sums0, sums1, sums2,
):
    gz, gy = lax.axis_index("gz"), lax.axis_index("gy")

    def load(i, src, dst, base):
        return pltpu.make_async_copy(src.at[pl.ds(16 * i, 16)], dst.at[pl.ds(16 * i, 16)], load_sems.at[base + i])

    weights = [
        pltpu.make_async_copy(src, dst, load_sems.at[8 + i])
        for i, (src, dst) in enumerate(
            ((w_value_in, w_value), (w_out_in, w_out), (w_query_in, w_query), (w_key_in, w_key))
        )
    ]
    for i in range(4):
        load(i, fields_in, fields, 0).start()
    for i in range(4):
        load(i, cot_in, cot, 4).start()
    for copy in weights:
        copy.start()

    barrier = pltpu.get_barrier_semaphore()

    def greet(device):
        pl.semaphore_signal(barrier, inc=1, device_id=device, device_id_type=MESH)

    each_device(greet, 0, 8)

    sum0[...] = jnp.zeros_like(sum0)
    for i in range(4):
        load(i, fields_in, fields, 0).wait()
        block = fields[pl.ds(16 * i, 16)].astype(F32)
        cells = jnp.sum(block, axis=1)
        sum0[pl.ds(Z + Y, X), :] += jnp.sum(block, axis=0)
        sum0[pl.ds(gz * ZL + i // 2, 1), :] += jnp.sum(cells, axis=0, keepdims=True)
        sum0[pl.ds(pl.multiple_of(Z + gy * YL + (i % 2) * 16, 16), 16), :] += cells
    means = Sum(sum0, pooled, near0, wide0, sums0)
    for i in range(4):
        load(i, cot_in, cot, 4).wait()
        cot_s[:, pl.ds(16 * i, 16), :] = jnp.swapaxes(cot[pl.ds(16 * i, 16)], 0, 1)
    for copy in weights:
        copy.wait()
    pl.semaphore_wait(barrier, 127)
    means.first()
    send(cot_s, cot_r, move_sems.at[0], move_sems.at[1], 0, 2)
    keep(cot_s, cot_r)
    means.second()
    send(cot_s, cot_r, move_sems.at[0], move_sems.at[1], 2, 4)
    means.third()
    send(cot_s, cot_r, move_sems.at[0], move_sems.at[1], 4, 8)

    def project_values(i, carry):
        start = pl.multiple_of(i * 16, 16)
        flat = fields[pl.ds(start, 16)].reshape(16 * X, C)
        values[pl.ds(start, 16)] = dot(flat, w_value[...]).astype(BF).reshape(16, X, C)
        return carry

    lax.fori_loop(0, 4, project_values, 0)
    means.end()

    attention(pooled, w_query, w_key, 2, attn_x, kernel_x, back_x)

    def over_x(i, carry):
        start = pl.multiple_of(i * 16, 16)
        for t in range(0, 16, 8):
            lines = mix(kernel_x, [values[start + t + n] for n in range(8)])
            for n in range(8):
                held[t + n] = lines[n]
        after_s[:, pl.ds(start, 16), :] = jnp.swapaxes(held[...], 0, 1)
        return carry

    lax.fori_loop(0, 4, over_x, 0)
    send(after_s, after_r, move_sems.at[2], move_sems.at[3])
    keep(after_s, after_r)
    attention(pooled, w_query, w_key, 0, attn_z, kernel_z, back_z)
    attention(pooled, w_query, w_key, 1, attn_y, kernel_y, back_y)
    means.close()

    wait_all(cot_r, move_sems.at[1])

    def back_over_z(step, carry):
        side, start = lax.div(step, 2), pl.multiple_of(lax.rem(step, 2) * 16, 16)
        y_start = pl.multiple_of(step * 16, 16)
        lines = []
        for low in range(ZL):
            lines.append(
                jnp.stack(
                    [cot_r[g * GY + side, pl.ds(low * YL + start, 16), :] for g in range(GZ)], axis=0
                )
            )
        block = jnp.stack(lines, axis=1).reshape(Z, 16, C)
        turned = jnp.swapaxes(block, 0, 1)
        cot_y[pl.ds(y_start, 16)] = turned
        grad_mixed = dot_nt(turned.reshape(16 * Z, C), w_out[...]).astype(BF).reshape(16, Z, C)
        mixed_y[pl.ds(y_start, 16)] = grad_mixed
        for t in range(0, 16, 8):
            lines = mix(back_z, [grad_mixed[t + n] for n in range(8)])
            for n in range(8):
                held[t + n, pl.ds(0, Z), :] = lines[n]
        grad_y[:, pl.ds(y_start, 16), :] = jnp.swapaxes(held[:, pl.ds(0, Z), :], 0, 1)
        return carry

    lax.fori_loop(0, 8, back_over_z, 0)

    def back_over_y(step, carry):
        lines = mix(back_y, [grad_y[step * 8 + n] for n in range(8)])
        for n in range(8):
            for side in range(GY):
                grad_s[(step * 4 + n // 2) * GY + side, pl.ds(n % 2 * YL, YL), :] = lines[n][
                    side * YL : (side + 1) * YL
                ]
        return carry

    lax.fori_loop(0, Z // 8, back_over_y, 0)
    halves = (pl.ds(0, YL), pl.ds(YL, YL))
    for low in range(ZL):
        send(grad_s, grad_r, move_sems.at[4], move_sems.at[5 + low], part=halves[low])
    keep(grad_s, grad_r)

    score_z[...] = jnp.zeros_like(score_z)
    score_y[...] = jnp.zeros_like(score_y)
    sum1[pl.ds(2 * (Z + Y), C), :] = jnp.zeros((C, C), F32)
    wait_all(after_r, move_sems.at[3])

    def over_y(step, carry):
        lines = []
        for n in range(8):
            lines.append(
                jnp.concatenate(
                    [after_r[(step * 4 + n // 2) * GY + side, pl.ds(n % 2 * YL, YL), :] for side in range(GY)], axis=0
                )
            )
        done = mix(kernel_y, lines)
        for n in range(8):
            after_y[step * 8 + n] = done[n]
        score_y[...] += pair_up([grad_y[step * 8 + n] for n in range(8)], lines)
        return carry

    lax.fori_loop(0, Z // 8, over_y, 0)

    def over_z(step, carry):
        y_start = pl.multiple_of(step * 16, 16)
        lines = jnp.swapaxes(after_y[:, pl.ds(y_start, 16), :], 0, 1)
        grad_mixed = mixed_y[pl.ds(y_start, 16)]
        parts = []
        for t in range(0, 16, 8):
            group = [lines[t + n] for n in range(8)]
            parts += mix(kernel_z, group)
            score_z[...] += pair_up([grad_mixed[t + n] for n in range(8)], group)
        mixed = jnp.concatenate(parts, axis=0)
        sum1[pl.ds(2 * (Z + Y), C), :] += dot_tn(mixed, cot_y[pl.ds(y_start, 16)].reshape(16 * Z, C))
        return carry

    lax.fori_loop(0, 8, over_z, 0)
    pull(pooled, w_query, w_key, 0, attn_z, score_z, sum1, 0, Z)
    pull(pooled, w_query, w_key, 1, attn_y, score_y, sum1, 2 * Z, 2 * Z + Y)
    early = Sum(sum1, total1, near1, wide1, sums1)
    early.first()

    score_x[...] = jnp.zeros_like(score_x)
    sum2[pl.ds(2 * X, C), :] = jnp.zeros((C, C), F32)

    def home(i, carry):
        start = pl.multiple_of(i * 16, 16)
        grad_x = jnp.swapaxes(grad_r[:, pl.ds(start, 16), :], 0, 1)
        for t in range(0, 16, 8):
            group = [grad_x[t + n] for n in range(8)]
            lines = mix(back_x, group)
            for n in range(8):
                grad_values[start + t + n] = lines[n]
            score_x[...] += pair_up(group, [values[start + t + n] for n in range(8)])
        grad = grad_values[pl.ds(start, 16)].reshape(16 * X, C)
        sum2[pl.ds(2 * X, C), :] += dot_tn(fields[pl.ds(start, 16)].reshape(16 * X, C), grad)
        return carry

    wait_all(grad_r, move_sems.at[5], halves[0])
    lax.fori_loop(0, 2, home, 0)
    early.second()
    wait_all(grad_r, move_sems.at[6], halves[1])
    lax.fori_loop(2, 4, home, 0)
    pull(pooled, w_query, w_key, 2, attn_x, score_x, sum2, 0, X)
    late = Sum(sum2, total2, near2, wide2, sums2)
    late.first()
    store_values = pltpu.make_async_copy(grad_values, grad_values_out, store_sems.at[0])
    store_values.start()
    early.third()
    late.second()
    early.end()
    early_rest[pl.ds(0, C), :] = total1[pl.ds(2 * (Z + Y), C), :]
    early_rest[pl.ds(5 * C, X), :] = pooled[pl.ds(Z + Y, X), :]
    early_rest[pl.ds(6 * C, Z), :] = settle(pooled, w_query, w_key, 0, total1, 0, Z, early_rest, C, 3 * C)
    early_rest[pl.ds(6 * C + Z, Y), :] = settle(
        pooled, w_query, w_key, 1, total1, 2 * Z, 2 * Z + Y, early_rest, 2 * C, 4 * C
    )
    late.third()
    store_early = pltpu.make_async_copy(early_rest, rest_out.at[pl.ds(3 * C, 7 * C + Z)], store_sems.at[1])
    store_early.start()
    late.end()
    store_late = pltpu.make_async_copy(total2, rest_out.at[pl.ds(0, 3 * C)], store_sems.at[2])
    store_late.start()
    wait_all(cot_s, move_sems.at[0])
    wait_all(after_s, move_sems.at[2])
    wait_all(grad_s, move_sems.at[4])
    early.close()
    late.close()
    store_values.wait()
    store_early.wait()
    store_late.wait()


REST = 10 * C + Z


def finish_kernel(
    grad_values_in, rest_in, w_value_in, w_query_in, w_key_in,
    field_grad, value_grad, out_grad, query_grad, key_grad,
    grad_values, rest, w_value, w_query, w_key, query_x, key_x, done, load_sems, store_sems,
):
    gz, gy = lax.axis_index("gz"), lax.axis_index("gy")
    loads = [
        pltpu.make_async_copy(rest_in, rest, load_sems.at[4]),
        pltpu.make_async_copy(w_query_in.at[pl.ds(2, 1)], w_query, load_sems.at[5]),
        pltpu.make_async_copy(w_key_in.at[pl.ds(2, 1)], w_key, load_sems.at[6]),
        pltpu.make_async_copy(w_value_in, w_value, load_sems.at[7]),
    ]

    def part(src, dst, i, sem):
        return pltpu.make_async_copy(src.at[pl.ds(16 * i, 16)], dst.at[pl.ds(16 * i, 16)], sem)

    for copy in loads:
        copy.start()
    for i in range(4):
        part(grad_values_in, grad_values, i, load_sems.at[i]).start()
    for copy in loads:
        copy.wait()

    def block(i):
        return rest.at[pl.ds(C * i, C)]

    stores = [
        pltpu.make_async_copy(block(2), value_grad, store_sems.at[4]),
        pltpu.make_async_copy(block(3), out_grad, store_sems.at[5]),
        pltpu.make_async_copy(block(4), query_grad.at[0], store_sems.at[6]),
        pltpu.make_async_copy(block(5), query_grad.at[1], store_sems.at[7]),
        pltpu.make_async_copy(block(6), key_grad.at[0], store_sems.at[8]),
        pltpu.make_async_copy(block(7), key_grad.at[1], store_sems.at[9]),
        pltpu.make_async_copy(query_x, query_grad.at[2], store_sems.at[10]),
        pltpu.make_async_copy(key_x, key_grad.at[2], store_sems.at[11]),
    ]
    for copy in stores[:6]:
        copy.start()
    means = rest[pl.ds(8 * C, X), :] / COUNTS[2]
    scale = lax.rsqrt(jnp.mean(means * means, axis=-1, keepdims=True) + EPS)
    normed = means * scale
    grad_q, grad_k = rest[pl.ds(0, X), :], rest[pl.ds(X, X), :]
    query_x[...] = dot_tn(normed, grad_q, HIGH)
    key_x[...] = dot_tn(normed, grad_k, HIGH)
    for copy in stores[6:]:
        copy.start()
    grad = dot_nt(grad_q, w_query[0], HIGH) + dot_nt(grad_k, w_key[0], HIGH)
    inner = jnp.mean(grad * normed, axis=-1, keepdims=True)
    means_x = scale * (grad - normed * inner) / COUNTS[2]
    for i in range(4):
        part(grad_values_in, grad_values, i, load_sems.at[i]).wait()
        direct = dot_nt(grad_values[pl.ds(16 * i, 16)].reshape(16 * X, C), w_value[...]).reshape(16, X, C)
        part_z = rest[pl.ds(9 * C + gz * ZL + i // 2, 1), :]
        part_y = rest[pl.ds(pl.multiple_of(9 * C + Z + gy * YL + (i % 2) * 16, 16), 16), :]
        cells = part_z + part_y
        done[pl.ds(16 * i, 16)] = (direct + cells[:, None, :] + means_x[None]).astype(BF)
        part(done, field_grad, i, store_sems.at[i]).start()
    for i in range(4):
        part(done, field_grad, i, store_sems.at[i]).wait()
    for copy in stores:
        copy.wait()


def local(fields, cotangent, w_value, w_out, w_query, w_key):
    hbm = pl.BlockSpec(memory_space=pltpu.HBM)
    cells = (CELLS, X, C)
    blocks = (X, CELLS, C)
    sums = []
    for rows in (POOLED, 2 * (Z + Y) + C, 2 * X + C):
        sums += [
            pltpu.VMEM((rows, C), F32),
            pltpu.VMEM((rows, C), F32),
            pltpu.VMEM((8, rows // 8, C), F32),
            pltpu.VMEM((16, rows // 8, C), F32),
        ]
    map_shapes = []
    for length in LENGTHS:
        map_shapes += [
            pltpu.VMEM((H * length, length), F32),
            pltpu.VMEM((length, H * length), BF),
            pltpu.VMEM((length, H * length), BF),
        ]
    field_shapes = [
        cells, cells, blocks, blocks, (Y, Z, C), (Y, Z, C), (Z, Y, C), blocks, blocks, blocks, (Z, Y, C), blocks,
        cells, cells,
    ]
    weights = [pltpu.VMEM((C, C), BF)] * 2 + [pltpu.VMEM((3, C, C), F32)] * 2
    grad_values, rest = pl.pallas_call(
        whole_kernel,
        in_specs=[hbm] * 6,
        out_specs=[hbm] * 2,
        out_shape=[jax.ShapeDtypeStruct(cells, BF), jax.ShapeDtypeStruct((REST, C), F32)],
        scratch_shapes=[pltpu.VMEM(shape, BF) for shape in field_shapes]
        + [pltpu.VMEM((16, X, C), BF)]
        + weights
        + map_shapes
        + [
            pltpu.VMEM((H * Z, Z), F32),
            pltpu.VMEM((H * Y, Y), F32),
            pltpu.VMEM((H * X, X), F32),
            pltpu.VMEM((7 * C + Z, C), F32),
        ]
        + sums
        + [pltpu.SemaphoreType.DMA((count,)) for count in (12, 3, 7, 6, 6, 6)],
        compiler_params=params(collective_id=0, has_side_effects=True),
    )(fields.reshape(cells), cotangent.reshape(cells), w_value, w_out, w_query, w_key)
    square = jax.ShapeDtypeStruct((C, C), F32)
    cube = jax.ShapeDtypeStruct((3, C, C), F32)
    field_grad, value_grad, out_grad, query_grad, key_grad = pl.pallas_call(
        finish_kernel,
        in_specs=[hbm] * 5,
        out_specs=[hbm] * 5,
        out_shape=[jax.ShapeDtypeStruct(cells, BF), square, square, cube, cube],
        scratch_shapes=[
            pltpu.VMEM(cells, BF),
            pltpu.VMEM((REST, C), F32),
            pltpu.VMEM((C, C), BF),
            pltpu.VMEM((1, C, C), F32),
            pltpu.VMEM((1, C, C), F32),
            pltpu.VMEM((C, C), F32),
            pltpu.VMEM((C, C), F32),
            pltpu.VMEM(cells, BF),
            pltpu.SemaphoreType.DMA((8,)),
            pltpu.SemaphoreType.DMA((12,)),
        ],
        compiler_params=params(),
    )(grad_values, rest, w_value, w_query, w_key)
    return (field_grad.reshape(ZL, YL, X, C), value_grad, out_grad, query_grad, key_grad)


def solution(mesh):
    placed = (P("gz", "gy", None, None), P("gz", "gy", None, None), P(), P(), P(), P())
    return jax.shard_map(
        local,
        mesh=mesh,
        in_specs=placed,
        out_specs=(P("gz", "gy", None, None), P(), P(), P(), P()),
        check_vma=False,
    )
```

time: 146 us -> 128 us (0.88)
  Pallas kernels: 139 us -> 127 us
  local copies, waits for them, and re-layouts: 5.84 us -> 0 us
    pallas_call x1 -> x2, Pallas kernels: 139 us -> 127 us  [the longest x1 122 us: local(): pl.pallas_call(whole_kernel, in_specs=[hbm] * 6, out_specs=[hbm] * 2, out...]
    unnamed x13 -> x0, local copies, waits for them, and re-layouts: 5.84 us -> none
where the time goes in v3:
time: 128 us
  Pallas kernels  127 us (99%)
    pallas_call x1, Pallas kernels, local(): pl.pallas_call(whole_kernel, in_specs=[hbm] * 6, out_specs=[hbm] * 2, out...  122 us
    pallas_call x1, Pallas kernels, local(): pl.pallas_call(finish_kernel, in_specs=[hbm] * 5, out_specs=[hbm] * 5, ou...  4.64 us

profile of v3, /device:TPU:1, one launch (start us, length us, event | category | flops | bytes accessed | tf_op | source)
XLA Modules:
  0.0 127.8 jit_solution(13791647343568120702)
XLA Ops:
  0.6 122.4 %shard_map.101 = (bf16[64,128,128]{2,1,0:T(8,128)(2,1)}, f32[1344,128]{1,0:T(8,128)}) custom-call(bf16[64,128,128]{2,1,0:T(8,128)(2,1)} %bitcast.3, bf16[64,128,128]{2,1,0:T(8,128)(2,1)} %bitcast.4, bf16[128,128]{1,0:T(8,128)(2,1)} %w_value_in.3, bf16[128,128]{1,0:T(8,128)(2,1)} %w_out_in.1, f32[3,128,128]{2,1,0:T(8,128)} %w_query_in.3, f32[3,128,128]{2,1,0:T(8,128)} %w_key_in.3), custom_call_target="tpu_custom_call" | custom-call | tf_op jit(solution)/shard_map/pallas_call | solution.py:548
  123.0 4.6 %shard_map.102 = (bf16[64,128,128]{2,1,0:T(8,128)(2,1)}, f32[128,128]{1,0:T(8,128)}, f32[128,128]{1,0:T(8,128)}, f32[3,128,128]{2,1,0:T(8,128)}, f32[3,128,128]{2,1,0:T(8,128)}) custom-call(bf16[64,128,128]{2,1,0:T(8,128)(2,1)} %get-tuple-element.12.grad_values_in, f32[1344,128]{1,0:T(8,128)} %get-tuple-element.13.rest_in, bf16[128,128]{1,0:T(8,128)(2,1)} %w_value_in.3, ...), custom_call_target="tpu_custom_call" | custom-call | tf_op jit(solution)/shard_map/pallas_call | solution.py:569

commit v4 on v3

--- a/solution.py
+++ b/solution.py
@@ -50,13 +50,39 @@
     return jnp.concatenate([jnp.where(head == h, block, zero) for h in range(H)], axis=0)
 
 
-def mix(kernel, lines):
-    done = dot(kernel[...], head_stack(jnp.concatenate(lines, axis=1))).astype(BF)
-    return [done[:, C * t : C * (t + 1)] for t in range(len(lines))]
-
-
-def pair_up(left, right):
-    return dot_nt(head_stack(jnp.concatenate(left, axis=1)), jnp.concatenate(right, axis=1))
+def regroup(lines):
+    group = lax.broadcasted_iota(jnp.int32, lines[0].shape, 1) // D
+    for s in (1, 2, 4):
+        low = group // s % 2 == 0
+        found = list(lines)
+        for k in range(8):
+            if k // s % 2 == 0:
+                a, b = lines[k], lines[k + s]
+                found[k] = jnp.where(low, a, pltpu.roll(b, D * s, 1))
+                found[k + s] = jnp.where(low, pltpu.roll(a, C - D * s, 1), b)
+        lines = found
+    return lines
+
+
+def to_heads(lines):
+    first, second = regroup(lines[:8]), regroup(lines[8:])
+    return [jnp.concatenate([a, b], axis=1) for a, b in zip(first, second)]
+
+
+def to_lines(heads):
+    return regroup([head[:, :C] for head in heads]) + regroup([head[:, C:] for head in heads])
+
+
+def mix(kernel, heads):
+    length = heads[0].shape[0]
+    done = [dot(kernel[h * length : (h + 1) * length], heads[h]).astype(BF) for h in range(H)]
+    return to_lines(done)
+
+
+def pair_up(score, left, right):
+    length = left[0].shape[0]
+    for h in range(H):
+        score[pl.ds(h * length, length), :] += dot_nt(left[h], right[h])
 
 
 def normalise(pooled, axis):
@@ -79,8 +105,8 @@
     soft = grown / jnp.sum(grown, axis=-1, keepdims=True)
     attn[...] = soft
     heads = [soft[h * length : (h + 1) * length] for h in range(H)]
-    kernel[...] = jnp.concatenate(heads, axis=1).astype(BF)
-    back[...] = jnp.concatenate([head.T for head in heads], axis=1).astype(BF)
+    kernel[...] = soft.astype(BF)
+    back[...] = jnp.concatenate([head.T for head in heads], axis=0).astype(BF)
 
 
 def pull(pooled, w_query, w_key, axis, attn, score, out, row_q, row_k):
@@ -246,7 +272,7 @@
     attn_z, kernel_z, back_z, attn_y, kernel_y, back_y, attn_x, kernel_x, back_x,
     score_z, score_y, score_x, early_rest,
     sum0, pooled, near0, wide0, sum1, total1, near1, wide1, sum2, total2, near2, wide2,
-    load_sems, store_sems, move_sems, sums0, sums1, sums2,
+    load_sems, store_sems, move_sems, sums0, sums1, sums2, group_in,
 ):
     gz, gy = lax.axis_index("gz"), lax.axis_index("gy")
 
@@ -266,12 +292,12 @@
     for copy in weights:
         copy.start()
 
+    means = Sum(sum0, pooled, near0, wide0, sums0)
     barrier = pltpu.get_barrier_semaphore()
-
-    def greet(device):
-        pl.semaphore_signal(barrier, inc=1, device_id=device, device_id_type=MESH)
-
-    each_device(greet, 0, 8)
+    for k in range(1, 8):
+        pl.semaphore_signal(barrier, inc=1, device_id=means.near_peer(k)[1], device_id_type=MESH)
+    for k in range(1, 16):
+        pl.semaphore_signal(barrier, inc=1, device_id=means.wide_peer(k)[1], device_id_type=MESH)
 
     sum0[...] = jnp.zeros_like(sum0)
     for i in range(4):
@@ -281,14 +307,14 @@
         sum0[pl.ds(Z + Y, X), :] += jnp.sum(block, axis=0)
         sum0[pl.ds(gz * ZL + i // 2, 1), :] += jnp.sum(cells, axis=0, keepdims=True)
         sum0[pl.ds(pl.multiple_of(Z + gy * YL + (i % 2) * 16, 16), 16), :] += cells
-    means = Sum(sum0, pooled, near0, wide0, sums0)
+    pl.semaphore_wait(barrier, 22)
+    means.first()
+    for k in range(1, 16):
+        pl.semaphore_signal(group_in, inc=1, device_id=means.wide_peer(k)[1], device_id_type=MESH)
     for i in range(4):
         load(i, cot_in, cot, 4).wait()
         cot_s[:, pl.ds(16 * i, 16), :] = jnp.swapaxes(cot[pl.ds(16 * i, 16)], 0, 1)
-    for copy in weights:
-        copy.wait()
-    pl.semaphore_wait(barrier, 127)
-    means.first()
+    pl.semaphore_wait(group_in, 15)
     send(cot_s, cot_r, move_sems.at[0], move_sems.at[1], 0, 2)
     keep(cot_s, cot_r)
     means.second()
@@ -296,6 +322,9 @@
     means.third()
     send(cot_s, cot_r, move_sems.at[0], move_sems.at[1], 4, 8)
 
+    for copy in weights:
+        copy.wait()
+
     def project_values(i, carry):
         start = pl.multiple_of(i * 16, 16)
         flat = fields[pl.ds(start, 16)].reshape(16 * X, C)
@@ -309,10 +338,9 @@
 
     def over_x(i, carry):
         start = pl.multiple_of(i * 16, 16)
-        for t in range(0, 16, 8):
-            lines = mix(kernel_x, [values[start + t + n] for n in range(8)])
-            for n in range(8):
-                held[t + n] = lines[n]
+        lines = mix(kernel_x, to_heads([values[start + n] for n in range(16)]))
+        for n in range(16):
+            held[n] = lines[n]
         after_s[:, pl.ds(start, 16), :] = jnp.swapaxes(held[...], 0, 1)
         return carry
 
@@ -340,25 +368,24 @@
         cot_y[pl.ds(y_start, 16)] = turned
         grad_mixed = dot_nt(turned.reshape(16 * Z, C), w_out[...]).astype(BF).reshape(16, Z, C)
         mixed_y[pl.ds(y_start, 16)] = grad_mixed
-        for t in range(0, 16, 8):
-            lines = mix(back_z, [grad_mixed[t + n] for n in range(8)])
-            for n in range(8):
-                held[t + n, pl.ds(0, Z), :] = lines[n]
+        lines = mix(back_z, to_heads([grad_mixed[n] for n in range(16)]))
+        for n in range(16):
+            held[n, pl.ds(0, Z), :] = lines[n]
         grad_y[:, pl.ds(y_start, 16), :] = jnp.swapaxes(held[:, pl.ds(0, Z), :], 0, 1)
         return carry
 
     lax.fori_loop(0, 8, back_over_z, 0)
 
     def back_over_y(step, carry):
-        lines = mix(back_y, [grad_y[step * 8 + n] for n in range(8)])
-        for n in range(8):
+        lines = mix(back_y, to_heads([grad_y[step * 16 + n] for n in range(16)]))
+        for n in range(16):
             for side in range(GY):
-                grad_s[(step * 4 + n // 2) * GY + side, pl.ds(n % 2 * YL, YL), :] = lines[n][
+                grad_s[(step * 8 + n // 2) * GY + side, pl.ds(n % 2 * YL, YL), :] = lines[n][
                     side * YL : (side + 1) * YL
                 ]
         return carry
 
-    lax.fori_loop(0, Z // 8, back_over_y, 0)
+    lax.fori_loop(0, Z // 16, back_over_y, 0)
     halves = (pl.ds(0, YL), pl.ds(YL, YL))
     for low in range(ZL):
         send(grad_s, grad_r, move_sems.at[4], move_sems.at[5 + low], part=halves[low])
@@ -371,30 +398,28 @@
 
     def over_y(step, carry):
         lines = []
-        for n in range(8):
+        for n in range(16):
             lines.append(
                 jnp.concatenate(
-                    [after_r[(step * 4 + n // 2) * GY + side, pl.ds(n % 2 * YL, YL), :] for side in range(GY)], axis=0
+                    [after_r[(step * 8 + n // 2) * GY + side, pl.ds(n % 2 * YL, YL), :] for side in range(GY)], axis=0
                 )
             )
-        done = mix(kernel_y, lines)
-        for n in range(8):
-            after_y[step * 8 + n] = done[n]
-        score_y[...] += pair_up([grad_y[step * 8 + n] for n in range(8)], lines)
-        return carry
-
-    lax.fori_loop(0, Z // 8, over_y, 0)
+        heads = to_heads(lines)
+        pair_up(score_y, to_heads([grad_y[step * 16 + n] for n in range(16)]), heads)
+        done = mix(kernel_y, heads)
+        for n in range(16):
+            after_y[step * 16 + n] = done[n]
+        return carry
+
+    lax.fori_loop(0, Z // 16, over_y, 0)
 
     def over_z(step, carry):
         y_start = pl.multiple_of(step * 16, 16)
         lines = jnp.swapaxes(after_y[:, pl.ds(y_start, 16), :], 0, 1)
         grad_mixed = mixed_y[pl.ds(y_start, 16)]
-        parts = []
-        for t in range(0, 16, 8):
-            group = [lines[t + n] for n in range(8)]
-            parts += mix(kernel_z, group)
-            score_z[...] += pair_up([grad_mixed[t + n] for n in range(8)], group)
-        mixed = jnp.concatenate(parts, axis=0)
+        heads = to_heads([lines[n] for n in range(16)])
+        pair_up(score_z, to_heads([grad_mixed[n] for n in range(16)]), heads)
+        mixed = jnp.concatenate(mix(kernel_z, heads), axis=0)
         sum1[pl.ds(2 * (Z + Y), C), :] += dot_tn(mixed, cot_y[pl.ds(y_start, 16)].reshape(16 * Z, C))
         return carry
 
@@ -410,20 +435,19 @@
     def home(i, carry):
         start = pl.multiple_of(i * 16, 16)
         grad_x = jnp.swapaxes(grad_r[:, pl.ds(start, 16), :], 0, 1)
-        for t in range(0, 16, 8):
-            group = [grad_x[t + n] for n in range(8)]
-            lines = mix(back_x, group)
-            for n in range(8):
-                grad_values[start + t + n] = lines[n]
-            score_x[...] += pair_up(group, [values[start + t + n] for n in range(8)])
+        heads = to_heads([grad_x[n] for n in range(16)])
+        pair_up(score_x, heads, to_heads([values[start + n] for n in range(16)]))
+        lines = mix(back_x, heads)
+        for n in range(16):
+            grad_values[start + n] = lines[n]
         grad = grad_values[pl.ds(start, 16)].reshape(16 * X, C)
         sum2[pl.ds(2 * X, C), :] += dot_tn(fields[pl.ds(start, 16)].reshape(16 * X, C), grad)
         return carry
 
     wait_all(grad_r, move_sems.at[5], halves[0])
     lax.fori_loop(0, 2, home, 0)
+    wait_all(grad_r, move_sems.at[6], halves[1])
     early.second()
-    wait_all(grad_r, move_sems.at[6], halves[1])
     lax.fori_loop(2, 4, home, 0)
     pull(pooled, w_query, w_key, 2, attn_x, score_x, sum2, 0, X)
     late = Sum(sum2, total2, near2, wide2, sums2)
@@ -537,8 +561,8 @@
     for length in LENGTHS:
         map_shapes += [
             pltpu.VMEM((H * length, length), F32),
-            pltpu.VMEM((length, H * length), BF),
-            pltpu.VMEM((length, H * length), BF),
+            pltpu.VMEM((H * length, length), BF),
+            pltpu.VMEM((H * length, length), BF),
         ]
     field_shapes = [
         cells, cells, blocks, blocks, (Y, Z, C), (Y, Z, C), (Z, Y, C), blocks, blocks, blocks, (Z, Y, C), blocks,
@@ -561,7 +585,8 @@
             pltpu.VMEM((7 * C + Z, C), F32),
         ]
         + sums
-        + [pltpu.SemaphoreType.DMA((count,)) for count in (12, 3, 7, 6, 6, 6)],
+        + [pltpu.SemaphoreType.DMA((count,)) for count in (12, 3, 7, 6, 6, 6)]
+        + [pltpu.SemaphoreType.REGULAR],
         compiler_params=params(collective_id=0, has_side_effects=True),
     )(fields.reshape(cells), cotangent.reshape(cells), w_value, w_out, w_query, w_key)
     square = jax.ShapeDtypeStruct((C, C), F32)

time: 128 us -> 129 us (level)
  no operation moved by 1% of the time
where the time goes in v4:
time: 129 us
  Pallas kernels  128 us (99%)
    pallas_call x1, Pallas kernels, local(): pl.pallas_call(whole_kernel, in_specs=[hbm] * 6, out_specs=[hbm] * 2, out...  123 us
    pallas_call x1, Pallas kernels, local(): pl.pallas_call(finish_kernel, in_specs=[hbm] * 5, out_specs=[hbm] * 5, ou...  4.64 us

profile of v4, /device:TPU:1, one launch (start us, length us, event | category | flops | bytes accessed | tf_op | source)
XLA Modules:
  0.0 128.8 jit_solution(6809378762764497328)
XLA Ops:
  0.6 123.3 %shard_map.101 = (bf16[64,128,128]{2,1,0:T(8,128)(2,1)}, f32[1344,128]{1,0:T(8,128)}) custom-call(bf16[64,128,128]{2,1,0:T(8,128)(2,1)} %bitcast.3, bf16[64,128,128]{2,1,0:T(8,128)(2,1)} %bitcast.4, bf16[128,128]{1,0:T(8,128)(2,1)} %w_value_in.3, bf16[128,128]{1,0:T(8,128)(2,1)} %w_out_in.1, f32[3,128,128]{2,1,0:T(8,128)} %w_query_in.3, f32[3,128,128]{2,1,0:T(8,128)} %w_key_in.3), custom_call_target="tpu_custom_call" | custom-call | tf_op jit(solution)/shard_map/pallas_call | solution.py:572
  124.0 4.6 %shard_map.102 = (bf16[64,128,128]{2,1,0:T(8,128)(2,1)}, f32[128,128]{1,0:T(8,128)}, f32[128,128]{1,0:T(8,128)}, f32[3,128,128]{2,1,0:T(8,128)}, f32[3,128,128]{2,1,0:T(8,128)}) custom-call(bf16[64,128,128]{2,1,0:T(8,128)(2,1)} %get-tuple-element.12.grad_values_in, f32[1344,128]{1,0:T(8,128)} %get-tuple-element.13.rest_in, bf16[128,128]{1,0:T(8,128)(2,1)} %w_value_in.3, ...), custom_call_target="tpu_custom_call" | custom-call | tf_op jit(solution)/shard_map/pallas_call | solution.py:594

commit v5 on v3

--- a/solution.py
+++ b/solution.py
@@ -50,13 +50,51 @@
     return jnp.concatenate([jnp.where(head == h, block, zero) for h in range(H)], axis=0)
 
 
+def head_of(shape):
+    return lax.broadcasted_iota(jnp.int32, shape, 1) % C // D
+
+
+def sides(length):
+    return 4 if length == Z else 2
+
+
+def arrange(heads):
+    g = sides(heads[0].shape[0])
+    return jnp.concatenate([jnp.concatenate(heads[p : p + g], axis=1) for p in range(0, H, g)], axis=0)
+
+
 def mix(kernel, lines):
-    done = dot(kernel[...], head_stack(jnp.concatenate(lines, axis=1))).astype(BF)
+    length = lines[0].shape[0]
+    g = sides(length)
+    block = jnp.concatenate(lines, axis=1)
+    head = head_of(block.shape)
+    zero = jnp.zeros((), BF)
+    deep = jnp.concatenate([jnp.where(head % g == r, block, zero) for r in range(g)], axis=0)
+    tall = dot(kernel[...], deep)
+    done = tall[:length]
+    for p in range(1, H // g):
+        done = jnp.where(head // g == p, tall[p * length : (p + 1) * length], done)
+    done = done.astype(BF)
     return [done[:, C * t : C * (t + 1)] for t in range(len(lines))]
 
 
 def pair_up(left, right):
-    return dot_nt(head_stack(jnp.concatenate(left, axis=1)), jnp.concatenate(right, axis=1))
+    g = sides(left[0].shape[0])
+    left, right = jnp.concatenate(left, axis=1), jnp.concatenate(right, axis=1)
+    head = head_of(left.shape)
+    zero = jnp.zeros((), BF)
+    tall = jnp.concatenate([jnp.where(head // g == p, left, zero) for p in range(H // g)], axis=0)
+    wide = jnp.concatenate([jnp.where(head % g == r, right, zero) for r in range(g)], axis=0)
+    return dot_nt(tall, wide)
+
+
+def apart(score, length):
+    g = sides(length)
+    heads = []
+    for h in range(H):
+        p, r = h // g, h % g
+        heads.append(score[p * length : (p + 1) * length, r * length : (r + 1) * length])
+    return jnp.concatenate(heads, axis=0)
 
 
 def normalise(pooled, axis):
@@ -79,8 +117,8 @@
     soft = grown / jnp.sum(grown, axis=-1, keepdims=True)
     attn[...] = soft
     heads = [soft[h * length : (h + 1) * length] for h in range(H)]
-    kernel[...] = jnp.concatenate(heads, axis=1).astype(BF)
-    back[...] = jnp.concatenate([head.T for head in heads], axis=1).astype(BF)
+    kernel[...] = arrange(heads).astype(BF)
+    back[...] = arrange([head.T for head in heads]).astype(BF)
 
 
 def pull(pooled, w_query, w_key, axis, attn, score, out, row_q, row_k):
@@ -88,7 +126,7 @@
     normed, _ = normalise(pooled, axis)
     queries = head_stack(project(normed, w_query[axis]))
     keys = head_stack(project(normed, w_key[axis]))
-    soft, grad = attn[...], score[...]
+    soft, grad = attn[...], apart(score[...], length)
     inner = jnp.sum(soft * grad, axis=-1, keepdims=True)
     grad = soft * (grad - inner) * (1.0 / D**0.5)
     heads = [grad[h * length : (h + 1) * length] for h in range(H)]
@@ -246,7 +284,7 @@
     attn_z, kernel_z, back_z, attn_y, kernel_y, back_y, attn_x, kernel_x, back_x,
     score_z, score_y, score_x, early_rest,
     sum0, pooled, near0, wide0, sum1, total1, near1, wide1, sum2, total2, near2, wide2,
-    load_sems, store_sems, move_sems, sums0, sums1, sums2,
+    load_sems, store_sems, move_sems, sums0, sums1, sums2, group_in,
 ):
     gz, gy = lax.axis_index("gz"), lax.axis_index("gy")
 
@@ -266,12 +304,12 @@
     for copy in weights:
         copy.start()
 
+    means = Sum(sum0, pooled, near0, wide0, sums0)
     barrier = pltpu.get_barrier_semaphore()
-
-    def greet(device):
-        pl.semaphore_signal(barrier, inc=1, device_id=device, device_id_type=MESH)
-
-    each_device(greet, 0, 8)
+    for k in range(1, 8):
+        pl.semaphore_signal(barrier, inc=1, device_id=means.near_peer(k)[1], device_id_type=MESH)
+    for k in range(1, 16):
+        pl.semaphore_signal(barrier, inc=1, device_id=means.wide_peer(k)[1], device_id_type=MESH)
 
     sum0[...] = jnp.zeros_like(sum0)
     for i in range(4):
@@ -281,20 +319,8 @@
         sum0[pl.ds(Z + Y, X), :] += jnp.sum(block, axis=0)
         sum0[pl.ds(gz * ZL + i // 2, 1), :] += jnp.sum(cells, axis=0, keepdims=True)
         sum0[pl.ds(pl.multiple_of(Z + gy * YL + (i % 2) * 16, 16), 16), :] += cells
-    means = Sum(sum0, pooled, near0, wide0, sums0)
-    for i in range(4):
-        load(i, cot_in, cot, 4).wait()
-        cot_s[:, pl.ds(16 * i, 16), :] = jnp.swapaxes(cot[pl.ds(16 * i, 16)], 0, 1)
     for copy in weights:
         copy.wait()
-    pl.semaphore_wait(barrier, 127)
-    means.first()
-    send(cot_s, cot_r, move_sems.at[0], move_sems.at[1], 0, 2)
-    keep(cot_s, cot_r)
-    means.second()
-    send(cot_s, cot_r, move_sems.at[0], move_sems.at[1], 2, 4)
-    means.third()
-    send(cot_s, cot_r, move_sems.at[0], move_sems.at[1], 4, 8)
 
     def project_values(i, carry):
         start = pl.multiple_of(i * 16, 16)
@@ -303,6 +329,21 @@
         return carry
 
     lax.fori_loop(0, 4, project_values, 0)
+    pl.semaphore_wait(barrier, 22)
+    means.first()
+    for k in range(1, 16):
+        pl.semaphore_signal(group_in, inc=1, device_id=means.wide_peer(k)[1], device_id_type=MESH)
+    for i in range(4):
+        load(i, cot_in, cot, 4).wait()
+        cot_s[:, pl.ds(16 * i, 16), :] = jnp.swapaxes(cot[pl.ds(16 * i, 16)], 0, 1)
+    pl.semaphore_wait(group_in, 15)
+    send(cot_s, cot_r, move_sems.at[0], move_sems.at[1], 0, 1)
+    keep(cot_s, cot_r)
+    means.second()
+    send(cot_s, cot_r, move_sems.at[0], move_sems.at[1], 1, 3)
+    means.third()
+    send(cot_s, cot_r, move_sems.at[0], move_sems.at[1], 3, 8)
+
     means.end()
 
     attention(pooled, w_query, w_key, 2, attn_x, kernel_x, back_x)
@@ -422,8 +463,8 @@
 
     wait_all(grad_r, move_sems.at[5], halves[0])
     lax.fori_loop(0, 2, home, 0)
+    wait_all(grad_r, move_sems.at[6], halves[1])
     early.second()
-    wait_all(grad_r, move_sems.at[6], halves[1])
     lax.fori_loop(2, 4, home, 0)
     pull(pooled, w_query, w_key, 2, attn_x, score_x, sum2, 0, X)
     late = Sum(sum2, total2, near2, wide2, sums2)
@@ -537,8 +578,8 @@
     for length in LENGTHS:
         map_shapes += [
             pltpu.VMEM((H * length, length), F32),
-            pltpu.VMEM((length, H * length), BF),
-            pltpu.VMEM((length, H * length), BF),
+            pltpu.VMEM((H // sides(length) * length, sides(length) * length), BF),
+            pltpu.VMEM((H // sides(length) * length, sides(length) * length), BF),
         ]
     field_shapes = [
         cells, cells, blocks, blocks, (Y, Z, C), (Y, Z, C), (Z, Y, C), blocks, blocks, blocks, (Z, Y, C), blocks,
@@ -555,13 +596,14 @@
         + weights
         + map_shapes
         + [
-            pltpu.VMEM((H * Z, Z), F32),
-            pltpu.VMEM((H * Y, Y), F32),
-            pltpu.VMEM((H * X, X), F32),
+            pltpu.VMEM((H // sides(Z) * Z, sides(Z) * Z), F32),
+            pltpu.VMEM((H // sides(Y) * Y, sides(Y) * Y), F32),
+            pltpu.VMEM((H // sides(X) * X, sides(X) * X), F32),
             pltpu.VMEM((7 * C + Z, C), F32),
         ]
         + sums
-        + [pltpu.SemaphoreType.DMA((count,)) for count in (12, 3, 7, 6, 6, 6)],
+        + [pltpu.SemaphoreType.DMA((count,)) for count in (12, 3, 7, 6, 6, 6)]
+        + [pltpu.SemaphoreType.REGULAR],
         compiler_params=params(collective_id=0, has_side_effects=True),
     )(fields.reshape(cells), cotangent.reshape(cells), w_value, w_out, w_query, w_key)
     square = jax.ShapeDtypeStruct((C, C), F32)

time: 128 us -> 119 us (0.930)
  Pallas kernels: 127 us -> 118 us
    pallas_call x1, Pallas kernels: 122 us -> 114 us  [local(): pl.pallas_call(whole_kernel, in_specs=[hbm] * 6, out_specs=[hbm] * 2, out...]
where the time goes in v5:
time: 119 us
  Pallas kernels  118 us (99%)
    pallas_call x1, Pallas kernels, local(): pl.pallas_call(whole_kernel, in_specs=[hbm] * 6, out_specs=[hbm] * 2, out...  114 us
    pallas_call x1, Pallas kernels, local(): pl.pallas_call(finish_kernel, in_specs=[hbm] * 5, out_specs=[hbm] * 5, ou...  4.64 us

profile of v5, /device:TPU:1, one launch (start us, length us, event | category | flops | bytes accessed | tf_op | source)
XLA Modules:
  0.0 119.1 jit_solution(17458937095562693916)
XLA Ops:
  0.6 113.7 %shard_map.101 = (bf16[64,128,128]{2,1,0:T(8,128)(2,1)}, f32[1344,128]{1,0:T(8,128)}) custom-call(bf16[64,128,128]{2,1,0:T(8,128)(2,1)} %bitcast.3, bf16[64,128,128]{2,1,0:T(8,128)(2,1)} %bitcast.4, bf16[128,128]{1,0:T(8,128)(2,1)} %w_value_in.3, bf16[128,128]{1,0:T(8,128)(2,1)} %w_out_in.1, f32[3,128,128]{2,1,0:T(8,128)} %w_query_in.3, f32[3,128,128]{2,1,0:T(8,128)} %w_key_in.3), custom_call_target="tpu_custom_call" | custom-call | tf_op jit(solution)/shard_map/pallas_call | solution.py:589
  114.3 4.6 %shard_map.102 = (bf16[64,128,128]{2,1,0:T(8,128)(2,1)}, f32[128,128]{1,0:T(8,128)}, f32[128,128]{1,0:T(8,128)}, f32[3,128,128]{2,1,0:T(8,128)}, f32[3,128,128]{2,1,0:T(8,128)}) custom-call(bf16[64,128,128]{2,1,0:T(8,128)(2,1)} %get-tuple-element.12.grad_values_in, f32[1344,128]{1,0:T(8,128)} %get-tuple-element.13.rest_in, bf16[128,128]{1,0:T(8,128)(2,1)} %w_value_in.3, ...), custom_call_target="tpu_custom_call" | custom-call | tf_op jit(solution)/shard_map/pallas_call | solution.py:611

commit v6 on v5

--- a/solution.py
+++ b/solution.py
@@ -16,6 +16,7 @@
 CELLS = ZL * YL
 GZ, GY = 32, 4
 EPS = 1e-06
+NEAR = (8, 16, 16)
 HIGH = lax.Precision.HIGHEST
 COUNTS = (Y * X, Z * X, Z * Y)
 STARTS = (0, Z, Z + Y)
@@ -225,21 +226,23 @@
 class Sum:
     def __init__(self, src, out, near, wide, sems):
         self.src, self.out, self.near, self.wide, self.sems = src, out, near, wide, sems
-        self.piece = src.shape[0] // 8
+        self.near_size, self.wide_size = near.shape[0], wide.shape[0]
+        self.piece = src.shape[0] // self.near_size
+        self.lows = self.near_size // 4
         gz, gy = lax.axis_index("gz"), lax.axis_index("gy")
-        self.gz, self.gy = gz, gy
-        self.line, self.side = lax.div(gz, 2), lax.rem(gz, 2) * 4 + gy
+        self.low, self.gy = lax.rem(gz, self.lows), gy
+        self.line, self.side = lax.div(gz, self.lows), self.low * 4 + gy
 
     def rows(self, index):
         return pl.ds(pl.multiple_of(index * self.piece, 8), self.piece)
 
     def near_peer(self, k):
-        peer = lax.rem(self.side + k, 8)
-        return peer, (self.line * 2 + lax.div(peer, 4), lax.rem(peer, 4))
+        peer = lax.rem(self.side + k, self.near_size)
+        return peer, (self.line * self.lows + lax.div(peer, 4), lax.rem(peer, 4))
 
     def wide_peer(self, k):
-        peer = lax.rem(self.line + k, 16)
-        return peer, (peer * 2 + lax.rem(self.gz, 2), self.gy)
+        peer = lax.rem(self.line + k, self.wide_size)
+        return peer, (peer * self.lows + self.low, self.gy)
 
     def copy(self, src, dst, first, device):
         pltpu.make_async_remote_copy(
@@ -247,33 +250,33 @@
         ).start()
 
     def first(self):
-        for k in range(1, 8):
+        for k in range(1, self.near_size):
             peer, device = self.near_peer(k)
             self.copy(self.src.at[self.rows(peer)], self.near.at[self.side], 0, device)
         self.near[self.side] = self.src[self.rows(self.side)]
 
     def second(self):
-        wait_bytes(self.near.at[pl.ds(0, 7)], self.sems.at[1])
+        wait_bytes(self.near.at[pl.ds(0, self.near_size - 1)], self.sems.at[1])
         self.wide[self.line] = jnp.sum(self.near[...], axis=0)
-        for k in range(1, 16):
+        for k in range(1, self.wide_size):
             peer, device = self.wide_peer(k)
             self.copy(self.wide.at[self.line], self.wide.at[self.line], 2, device)
 
     def third(self):
-        wait_bytes(self.wide.at[pl.ds(0, 15)], self.sems.at[3])
+        wait_bytes(self.wide.at[pl.ds(0, self.wide_size - 1)], self.sems.at[3])
         rows = self.rows(self.side)
         self.out[rows] = jnp.sum(self.wide[...], axis=0)
-        for k in range(1, 8):
+        for k in range(1, self.near_size):
             peer, device = self.near_peer(k)
             self.copy(self.out.at[rows], self.out.at[rows], 4, device)
 
     def end(self):
-        wait_bytes(self.near.at[pl.ds(0, 7)], self.sems.at[5])
+        wait_bytes(self.near.at[pl.ds(0, self.near_size - 1)], self.sems.at[5])
 
     def close(self):
-        wait_bytes(self.near.at[pl.ds(0, 7)], self.sems.at[0])
-        wait_bytes(self.wide.at[pl.ds(0, 15)], self.sems.at[2])
-        wait_bytes(self.near.at[pl.ds(0, 7)], self.sems.at[4])
+        wait_bytes(self.near.at[pl.ds(0, self.near_size - 1)], self.sems.at[0])
+        wait_bytes(self.wide.at[pl.ds(0, self.wide_size - 1)], self.sems.at[2])
+        wait_bytes(self.near.at[pl.ds(0, self.near_size - 1)], self.sems.at[4])
 
 
 def whole_kernel(
@@ -310,6 +313,10 @@
         pl.semaphore_signal(barrier, inc=1, device_id=means.near_peer(k)[1], device_id_type=MESH)
     for k in range(1, 16):
         pl.semaphore_signal(barrier, inc=1, device_id=means.wide_peer(k)[1], device_id_type=MESH)
+    other = lax.div(gz, 4) * 4 + 2 - lax.div(lax.rem(gz, 4), 2) * 2
+    for k in range(1, 8):
+        device = (other + lax.rem(lax.rem(gz, 2) + k // 4, 2), lax.rem(gy + k % 4, 4))
+        pl.semaphore_signal(barrier, inc=1, device_id=device, device_id_type=MESH)
 
     sum0[...] = jnp.zeros_like(sum0)
     for i in range(4):
@@ -329,7 +336,7 @@
         return carry
 
     lax.fori_loop(0, 4, project_values, 0)
-    pl.semaphore_wait(barrier, 22)
+    pl.semaphore_wait(barrier, 29)
     means.first()
     for k in range(1, 16):
         pl.semaphore_signal(group_in, inc=1, device_id=means.wide_peer(k)[1], device_id_type=MESH)
@@ -464,15 +471,16 @@
     wait_all(grad_r, move_sems.at[5], halves[0])
     lax.fori_loop(0, 2, home, 0)
     wait_all(grad_r, move_sems.at[6], halves[1])
+    lax.fori_loop(2, 4, home, 0)
     early.second()
-    lax.fori_loop(2, 4, home, 0)
     pull(pooled, w_query, w_key, 2, attn_x, score_x, sum2, 0, X)
     late = Sum(sum2, total2, near2, wide2, sums2)
     late.first()
     store_values = pltpu.make_async_copy(grad_values, grad_values_out, store_sems.at[0])
     store_values.start()
+    late.second()
     early.third()
-    late.second()
+    late.third()
     early.end()
     early_rest[pl.ds(0, C), :] = total1[pl.ds(2 * (Z + Y), C), :]
     early_rest[pl.ds(5 * C, X), :] = pooled[pl.ds(Z + Y, X), :]
@@ -480,7 +488,6 @@
     early_rest[pl.ds(6 * C + Z, Y), :] = settle(
         pooled, w_query, w_key, 1, total1, 2 * Z, 2 * Z + Y, early_rest, 2 * C, 4 * C
     )
-    late.third()
     store_early = pltpu.make_async_copy(early_rest, rest_out.at[pl.ds(3 * C, 7 * C + Z)], store_sems.at[1])
     store_early.start()
     late.end()
@@ -567,12 +574,12 @@
     cells = (CELLS, X, C)
     blocks = (X, CELLS, C)
     sums = []
-    for rows in (POOLED, 2 * (Z + Y) + C, 2 * X + C):
+    for rows, near in zip((POOLED, 2 * (Z + Y) + C, 2 * X + C), NEAR):
         sums += [
             pltpu.VMEM((rows, C), F32),
             pltpu.VMEM((rows, C), F32),
-            pltpu.VMEM((8, rows // 8, C), F32),
-            pltpu.VMEM((16, rows // 8, C), F32),
+            pltpu.VMEM((near, rows // near, C), F32),
+            pltpu.VMEM((128 // near, rows // near, C), F32),
         ]
     map_shapes = []
     for length in LENGTHS:

time: 119 us -> 118 us (level)
  no operation moved by 1% of the time
where the time goes in v6:
time: 118 us
  Pallas kernels  117 us (99%)
    pallas_call x1, Pallas kernels, local(): pl.pallas_call(whole_kernel, in_specs=[hbm] * 6, out_specs=[hbm] * 2, out...  113 us
    pallas_call x1, Pallas kernels, local(): pl.pallas_call(finish_kernel, in_specs=[hbm] * 5, out_specs=[hbm] * 5, ou...  4.64 us

profile of v6, /device:TPU:1, one launch (start us, length us, event | category | flops | bytes accessed | tf_op | source)
XLA Modules:
  0.0 118.2 jit_solution(11598013918607590863)
XLA Ops:
  0.6 112.8 %shard_map.101 = (bf16[64,128,128]{2,1,0:T(8,128)(2,1)}, f32[1344,128]{1,0:T(8,128)}) custom-call(bf16[64,128,128]{2,1,0:T(8,128)(2,1)} %bitcast.3, bf16[64,128,128]{2,1,0:T(8,128)(2,1)} %bitcast.4, bf16[128,128]{1,0:T(8,128)(2,1)} %w_value_in.3, bf16[128,128]{1,0:T(8,128)(2,1)} %w_out_in.1, f32[3,128,128]{2,1,0:T(8,128)} %w_query_in.3, f32[3,128,128]{2,1,0:T(8,128)} %w_key_in.3), custom_call_target="tpu_custom_call" | custom-call | tf_op jit(solution)/shard_map/pallas_call | solution.py:596
  113.4 4.6 %shard_map.102 = (bf16[64,128,128]{2,1,0:T(8,128)(2,1)}, f32[128,128]{1,0:T(8,128)}, f32[128,128]{1,0:T(8,128)}, f32[3,128,128]{2,1,0:T(8,128)}, f32[3,128,128]{2,1,0:T(8,128)}) custom-call(bf16[64,128,128]{2,1,0:T(8,128)(2,1)} %get-tuple-element.12.grad_values_in, f32[1344,128]{1,0:T(8,128)} %get-tuple-element.13.rest_in, bf16[128,128]{1,0:T(8,128)(2,1)} %w_value_in.3, ...), custom_call_target="tpu_custom_call" | custom-call | tf_op jit(solution)/shard_map/pallas_call | solution.py:618

commit v7 on v6

--- a/solution.py
+++ b/solution.py
@@ -161,8 +161,8 @@
 
 def shifts(step, first=0):
     lines, x, core = torus()
-    to_core = lax.rem(core + lax.rem(step, 2), 2)
-    turn = x + lax.div(step, 2)
+    to_core = lax.rem(core + lax.div(step, 4), 2)
+    turn = x + lax.rem(step, 4)
     sides = []
     for dx in range(4):
         to_x = lax.rem(turn + dx, 4)

time: 118 us -> 117 us (level)
  no operation moved by 1% of the time
where the time goes in v7:
time: 117 us
  Pallas kernels  116 us (99%)
    pallas_call x1, Pallas kernels, local(): pl.pallas_call(whole_kernel, in_specs=[hbm] * 6, out_specs=[hbm] * 2, out...  112 us
    pallas_call x1, Pallas kernels, local(): pl.pallas_call(finish_kernel, in_specs=[hbm] * 5, out_specs=[hbm] * 5, ou...  4.64 us

profile of v7, /device:TPU:1, one launch (start us, length us, event | category | flops | bytes accessed | tf_op | source)
XLA Modules:
  0.0 117.3 jit_solution(8079059940849090488)
XLA Ops:
  0.6 111.8 %shard_map.101 = (bf16[64,128,128]{2,1,0:T(8,128)(2,1)}, f32[1344,128]{1,0:T(8,128)}) custom-call(bf16[64,128,128]{2,1,0:T(8,128)(2,1)} %bitcast.3, bf16[64,128,128]{2,1,0:T(8,128)(2,1)} %bitcast.4, bf16[128,128]{1,0:T(8,128)(2,1)} %w_value_in.3, bf16[128,128]{1,0:T(8,128)(2,1)} %w_out_in.1, f32[3,128,128]{2,1,0:T(8,128)} %w_query_in.3, f32[3,128,128]{2,1,0:T(8,128)} %w_key_in.3), custom_call_target="tpu_custom_call" | custom-call | tf_op jit(solution)/shard_map/pallas_call | solution.py:596
  112.5 4.6 %shard_map.102 = (bf16[64,128,128]{2,1,0:T(8,128)(2,1)}, f32[128,128]{1,0:T(8,128)}, f32[128,128]{1,0:T(8,128)}, f32[3,128,128]{2,1,0:T(8,128)}, f32[3,128,128]{2,1,0:T(8,128)}) custom-call(bf16[64,128,128]{2,1,0:T(8,128)(2,1)} %get-tuple-element.12.grad_values_in, f32[1344,128]{1,0:T(8,128)} %get-tuple-element.13.rest_in, bf16[128,128]{1,0:T(8,128)(2,1)} %w_value_in.3, ...), custom_call_target="tpu_custom_call" | custom-call | tf_op jit(solution)/shard_map/pallas_call | solution.py:618
